TPU v7x, 128 devices: a whole 4x4x4 slice. The times are simulated.
128 devices in a mesh: row: 4 (over x_lo, core), col: 32 (over z, x_hi, y).
Axes of the slice: x: 4 (x_hi: 2, x_lo: 2; x = x_hi * 2 + x_lo), y: 4, z: 4, core: 2. Of those that a mesh axis runs over, the one named last changes fastest.
Arguments:
- schur: float32 [4096, 16384], P('row', 'col'), may hold values from -6 to 6
- left_rot: float32 [8, 512, 512], P('row', 'col'), may hold values from -1 to 1, as said below
- right_rot: float32 [32, 512, 512], P('col', 'row'), may hold values from -1 to 1, as said below
- left_off: float32 [8, 512, 512], P('row', 'col'), may hold values from -1 to 1, as said below
- right_off: float32 [32, 512, 512], P('col', 'row'), may hold values from -1 to 1, as said below
Outputs:
- updated: float32 [4096, 16384], P('row', 'col')
Inputs may be any that keep to these rules, and one draw needn't show every extreme that they name: `left_rot`: each 512 x 512 block is orthogonal. `right_rot`: each 512 x 512 block is orthogonal. `left_off`: each 512 x 512 block is orthogonal. `right_off`: each 512 x 512 block is orthogonal.
All inputs are finite; a program needn't handle non-finite values.
Results may differ from a plain program's by a relative error of at most 0.00007.
Values sent between devices are 32-bit elements; how exact they have to be, the bound alone decides.
No kernel may reach another device: no remote copies, remote signals or barrier semaphores. Data moves between devices by JAX's collectives and lax.ppermute only.
A program may use at most 64 MiB of HBM per device.

v0:
```python
import jax
import jax.numpy as jnp
from jax import lax
from jax.sharding import PartitionSpec as P


def passed_along(x, axis, by):
    size = lax.axis_size(axis)
    return lax.ppermute(x, axis, [(i, (i + by) % size) for i in range(size)])


def padded_2(cells, sides, width):
    for axis, dim in sides:
        count = lax.axis_size(axis)
        head = lax.slice_in_dim(cells, 0, width, axis=dim)
        tail = lax.slice_in_dim(cells, cells.shape[dim] - width, cells.shape[dim], axis=dim)
        cells = jnp.concatenate(
            [
                lax.ppermute(tail, axis, [(i, (i + 1) % count) for i in range(count)]),
                cells,
                lax.ppermute(head, axis, [((i + 1) % count, i) for i in range(count)]),
            ],
            axis=dim,
        )
    return cells


def apply_left(blocks, rotations):
    number = rotations.shape[0]
    window = rotations.shape[1]
    shaped = blocks.reshape(number, window, blocks.shape[1])
    result = jnp.einsum("kab,kac->kbc", rotations, shaped, precision=lax.Precision.HIGHEST)
    return result.reshape(number * window, blocks.shape[1])


def apply_right(blocks, rotations):
    number = rotations.shape[0]
    window = rotations.shape[1]
    shaped = blocks.reshape(blocks.shape[0], number, window)
    result = jnp.einsum("rka,kab->rkb", shaped, rotations, precision=lax.Precision.HIGHEST)
    return result.reshape(blocks.shape[0], number * window)


def body(schur, left_rot, right_rot, left_off, right_off):
    window = left_rot.shape[2]
    half_window = window // 2
    rows_here = schur.shape[0]
    cols_here = schur.shape[1]
    rotations = lax.all_gather(left_rot, "col", axis=1, tiled=True)
    matrix = apply_left(schur, rotations)
    rotations = lax.all_gather(right_rot, "row", axis=1, tiled=True)
    matrix = apply_right(matrix, rotations)
    rotations = lax.all_gather(left_off, "col", axis=1, tiled=True)
    following = passed_along(rotations[0][:, :half_window], "row", -1)
    padded = padded_2(matrix, (("row", 0),), half_window)
    leading = jnp.dot(
        rotations[0][:, half_window:].T, padded[:window], precision=lax.Precision.HIGHEST
    )
    middle = apply_left(padded[window:rows_here], rotations[1:])
    trailing = jnp.dot(
        following.T, padded[rows_here : rows_here + window], precision=lax.Precision.HIGHEST
    )
    matrix = jnp.concatenate([leading, middle, trailing], axis=0)
    rotations = lax.all_gather(right_off, "row", axis=1, tiled=True)
    following = passed_along(rotations[0][:, :half_window], "col", -1)
    padded = padded_2(matrix, (("col", 1),), half_window)
    leading = jnp.dot(
        padded[:, :window], rotations[0][:, half_window:], precision=lax.Precision.HIGHEST
    )
    middle = apply_right(padded[:, window:cols_here], rotations[1:])
    trailing = jnp.dot(
        padded[:, cols_here : cols_here + window], following, precision=lax.Precision.HIGHEST
    )
    return jnp.concatenate([leading, middle, trailing], axis=1)


def solution(mesh):
    return jax.shard_map(
        body,
        mesh=mesh,
        in_specs=(
            P("row", "col"),
            P("row", "col", None),
            P("col", "row", None),
            P("row", "col", None),
            P("col", "row", None),
        ),
        out_specs=P("row", "col"),
        check_vma=False,
    )
```

profile of v0, /device:TPU:0, one launch (start us, length us, event | category | flops | bytes accessed | tf_op | source)
XLA Modules:
  0.0 249.2 jit_solution(17795452879531469590)
XLA Ops:
  6.5 0.7 all-gather.5.cloned.1.call-update
  7.3 0.7 all-gather.7.cloned.1.call-update
  8.1 0.7 all-gather.9.cloned.1.call-update
  8.8 0.5 all-gather.11.cloned.1.call-update
  9.3 74.9 %all-gather.5.cloned.1.call-done = f32[2,512,512]{2,1,0:T(8,128)} async-done(((f32[2,16,512]{2,1,0:T(8,128)}), f32[2,512,512]{2,1,0:T(8,128)}) %all-gather.5.cloned.1.call-update) | async-done | bytes 2097168 | tf_op jit(solution)/shard_map/all_gather | solution.py:49
  84.2 6.4 %fusion.15 = f32[2,512,512]{2,1,0:T(8,128)} fusion(f32[2,512,512]{2,1,0:T(8,128)} %all-gather.5.cloned.1.call-done, f32[2,512,512]{2,1,0:T(8,128)S(1)} %bitcast.34), kind=kOutput, calls=%fused_computation.33 | convolution fusion | flops 3221225472 | bytes 6291456 | tf_op jit(solution)/shard_map/kab,kac->kbc/dot_general | solution.py:32
  90.6 13.7 %all-gather.7.cloned.1.call-done = f32[1,512,512]{2,1,0:T(8,128)} async-done(((f32[1,128,512]{2,1,0:T(8,128)}), f32[1,512,512]{2,1,0:T(8,128)}) %all-gather.7.cloned.1.call-update) | async-done | bytes 1048592 | tf_op jit(solution)/shard_map/all_gather | solution.py:51
  104.4 5.3 %fusion.6 = f32[1024,512]{1,0:T(8,128)S(1)} fusion(f32[1024,512]{1,0:T(8,128)} %bitcast.37, f32[1,512,512]{2,1,0:T(8,128)} %all-gather.7.cloned.1.call-done), kind=kOutput, calls=%fused_computation.22 | convolution fusion | flops 3221225472 | bytes 5242880 | tf_op jit(solution)/shard_map/rka,kab->rkb/dot_general | solution.py:40
  109.7 1.3 copy-done.1
  111.0 1.0 slice_bitcast_fusion.6
  112.1 0.3 collective-permute-start
  112.3 1.5 collective-permute-start.1
  113.8 65.9 %all-gather.9.cloned.1.call-done = f32[2,512,512]{2,1,0:T(8,128)} async-done(((f32[2,16,512]{2,1,0:T(8,128)}), f32[2,512,512]{2,1,0:T(8,128)}) %all-gather.9.cloned.1.call-update) | async-done | bytes 2097168 | tf_op jit(solution)/shard_map/all_gather | solution.py:53
  179.7 1.4 slice_bitcast_fusion.4
  181.2 0.3 collective-permute-start.2
  181.6 3.1 %convolution_bitcast_fusion = f32[512,512]{1,0:T(8,128)S(1)} fusion(f32[2,512,512]{2,1,0:T(8,128)} %all-gather.9.cloned.1.call-done, f32[1024,1,512]{2,0,1:T(8,128)S(1)} %bitcast.36), kind=kOutput, calls=%fused_computation.12 | convolution fusion | flops 1610612736 | bytes 3145728 | tf_op jit(solution)/shard_map/kab,kac->kbc/dot_general | solution.py:32
  184.8 2.2 convolution_bitcast_fusion.2
  186.9 1.3 collective-permute-done.2
  188.2 2.2 convolution_bitcast_fusion.1
  190.4 0.2 pad_maximum_fusion.12
  190.6 0.6 copy-done.5
  191.2 1.5 fusion.14
  192.7 0.3 collective-permute-start.3
  193.0 7.5 %collective-permute-start.4 = (f32[1024,256]{1,0:T(8,128)}, f32[1024,256]{1,0:T(8,128)}, u32[]{:S(2)}, u32[]{:S(2)}) collective-permute-start(f32[1024,256]{1,0:T(8,128)} %get-tuple-element.6), channel_id=1, source_target_pairs={{1,0},{2,1},{3,2},{4,3},{5,4},{6,5},{7,6},{8,7},{9,8},{10,9},{11,1... | collective-permute-start | bytes 3145736 | tf_op jit(solution)/shard_map/ppermute | solution.py:21
  200.4 1.1 slice.84
  201.5 9.8 %collective-permute-start.5 = (f32[512,256]{1,0:T(8,128)S(1)}, f32[512,256]{1,0:T(8,128)S(1)}, u32[]{:S(2)}, u32[]{:S(2)}) collective-permute-start(f32[512,256]{1,0:T(8,128)S(1)} %slice.84), channel_id=1, source_target_pairs={{0,31},{1,0},{2,1},{3,2},{4,3},{5,4},{6,5},{7,6},{8,7},{9,8},{10,9... | collective-permute-start | bytes 1572872 | tf_op jit(solution)/shard_map/ppermute | solution.py:9
  211.3 17.1 %collective-permute-done.3 = f32[1024,256]{1,0:T(8,128)} collective-permute-done((f32[1024,256]{1,0:T(8,128)}, f32[1024,256]{1,0:T(8,128)}, u32[]{:S(2)}, u32[]{:S(2)}) %collective-permute-start.3) | collective-permute-done | bytes 1048608 | tf_op jit(solution)/shard_map/ppermute | solution.py:19
  228.5 3.5 %fusion.2 = f32[1024,256]{0,1:T(8,128)S(1)} fusion(f32[1024,256]{1,0:T(8,128)} %collective-permute-done.3, f32[256,512]{1,0:T(8,128)} %copy-done.5, f32[512,512]{1,0:T(8,128)S(1)} %convolution_bitcast_fusion, f32[256,512]{1,0:T(8,128)} %copy-done.3, f32[512,512]{1,0:T(8,128)} %bitcast.39), kind=kOutput, calls=%fused_computation.6 | convolution fusion | flops 1612185600 | bytes 4718592 | tf_op jit(solution)/shard_map/dot_general | solution.py:67
  232.0 3.1 %collective-permute-done.5 = f32[512,256]{1,0:T(8,128)S(1)} collective-permute-done((f32[512,256]{1,0:T(8,128)S(1)}, f32[512,256]{1,0:T(8,128)S(1)}, u32[]{:S(2)}, u32[]{:S(2)}) %collective-permute-start.5) | collective-permute-done | bytes 524320 | tf_op jit(solution)/shard_map/ppermute | solution.py:9
  235.0 3.3 %fusion = f32[1024,256]{0,1:T(8,128)S(1)} fusion(f32[512,256]{1,0:T(8,128)S(1)} %collective-permute-done.5, f32[1024,256]{1,0:T(8,128)} %collective-permute-done.4, f32[256,512]{1,0:T(8,128)S(1)} %copy-done.6, f32[512,512]{1,0:T(8,128)S(1)} %convolution_bitcast_fusion, f32[256,512]{1,0:T(8,128)S(1)} %copy-done.4), kind=kOutput, calls=%fused_computation.1 | convolution fusion | flops 1612185600 | bytes 4718592 | tf_op jit(solution)/shard_map/dot_general | solution.py:71
  238.3 1.5 pad_maximum_fusion.13
  239.8 2.9 %copy.6 = f32[1024,512]{1,0:T(8,128)} copy(f32[1024,512]{0,1:T(8,128)} %pad_maximum_fusion.13) | data formatting | bytes 4194304 | tf_op jit(solution)/shard_map/concatenate | solution.py:74
  (21 shorter events, 0.3 us)
Async XLA Ops:
  6.5 77.7 %copy-start = (f32[1024,512]{1,0:T(8,128)S(1)}, f32[1024,512]{1,0:T(8,128)}, u32[]{:S(2)}) copy-start(f32[1024,512]{1,0:T(8,128)} %param.5) | copy-start | bytes 6291460
  6.5 77.7 %all-gather.5.cloned.1.call-start = ((), (), s32[]{:S(2)}) async-start(), calls=%async_computation | async-start | bytes 2162688 | tf_op jit(solution)/shard_map/all_gather | solution.py:49
  7.3 97.1 %all-gather.7.cloned.1.call-start = ((), (), s32[]{:S(2)}) async-start(), calls=%async_computation.1 | async-start | bytes 1310720 | tf_op jit(solution)/shard_map/all_gather | solution.py:51
  8.0 171.7 %all-gather.9.cloned.1.call-start = ((), (), s32[]{:S(2)}) async-start(), calls=%async_computation.2 | async-start | bytes 2162688 | tf_op jit(solution)/shard_map/all_gather | solution.py:53
  8.7 191.7 %all-gather.11.cloned.1.call-start = ((), (), s32[]{:S(2)}) async-start(), calls=%async_computation.3 | async-start | bytes 1310720 | tf_op jit(solution)/shard_map/all_gather | solution.py:64
  109.7 1.3 copy-start.1
  112.1 72.7 %collective-permute-start = (f32[256,512]{1,0:T(8,128)}, f32[256,512]{1,0:T(8,128)}, u32[]{:S(2)}, u32[]{:S(2)}) collective-permute-start(f32[256,512]{1,0:T(8,128)} %get-tuple-element.7), channel_id=1, source_target_pairs={{0,32},{32,64},{64,96},{96,0},{1,33},{33,65},{65,97},{97,1},{2,34}... | collective-permute-start | bytes 1572872 | tf_op jit(solution)/shard_map/ppermute | solution.py:19
  112.3 74.6 %collective-permute-start.1 = (f32[256,512]{1,0:T(8,128)}, f32[256,512]{1,0:T(8,128)}, u32[]{:S(2)}, u32[]{:S(2)}) collective-permute-start(f32[256,512]{1,0:T(8,128)} %get-tuple-element.8), channel_id=1, source_target_pairs={{32,0},{64,32},{96,64},{0,96},{33,1},{65,33},{97,65},{1,97},{34,2}... | collective-permute-start | bytes 1572872 | tf_op jit(solution)/shard_map/ppermute | solution.py:21
  179.7 1.9 copy-start.2
  181.2 7.0 %collective-permute-start.2 = (f32[512,256]{1,0:T(8,128)S(1)}, f32[512,256]{1,0:T(8,128)S(1)}, u32[]{:S(2)}, u32[]{:S(2)}) collective-permute-start(f32[512,256]{1,0:T(8,128)S(1)} %slice.80), channel_id=1, source_target_pairs={{0,96},{32,0},{64,32},{96,64},{1,97},{33,1},{65,33},{97,65},{2,98}... | collective-permute-start | bytes 1572872 | tf_op jit(solution)/shard_map/ppermute | solution.py:9
  186.9 3.7 %copy-start.3 = (f32[256,512]{1,0:T(8,128)}, f32[256,512]{1,0:T(8,128)S(1)}, u32[]{:S(2)}) copy-start(f32[256,512]{1,0:T(8,128)S(1)} %convolution_bitcast_fusion.2) | copy-start | bytes 1572868
  190.4 0.8 copy-start.5
  192.7 35.8 %collective-permute-start.3 = (f32[1024,256]{1,0:T(8,128)}, f32[1024,256]{1,0:T(8,128)}, u32[]{:S(2)}, u32[]{:S(2)}) collective-permute-start(f32[1024,256]{1,0:T(8,128)} %get-tuple-element.5), channel_id=1, source_target_pairs={{0,1},{1,2},{2,3},{3,4},{4,5},{5,6},{6,7},{7,8},{8,9},{9,10},{10,1... | collective-permute-start | bytes 3145736 | tf_op jit(solution)/shard_map/ppermute | solution.py:19
  193.0 42.1 %collective-permute-start.4 = (f32[1024,256]{1,0:T(8,128)}, f32[1024,256]{1,0:T(8,128)}, u32[]{:S(2)}, u32[]{:S(2)}) collective-permute-start(f32[1024,256]{1,0:T(8,128)} %get-tuple-element.6), channel_id=1, source_target_pairs={{1,0},{2,1},{3,2},{4,3},{5,4},{6,5},{7,6},{8,7},{9,8},{10,9},{11,1... | collective-permute-start | bytes 3145736 | tf_op jit(solution)/shard_map/ppermute | solution.py:21
  201.5 33.5 %copy-start.4 = (f32[256,512]{1,0:T(8,128)S(1)}, f32[256,512]{1,0:T(8,128)}, u32[]{:S(2)}) copy-start(f32[256,512]{1,0:T(8,128)} %copy-done.3) | copy-start | bytes 1572868
  201.5 33.5 %copy-start.6 = (f32[256,512]{1,0:T(8,128)S(1)}, f32[256,512]{1,0:T(8,128)}, u32[]{:S(2)}) copy-start(f32[256,512]{1,0:T(8,128)} %copy-done.5) | copy-start | bytes 1572868
  201.5 33.5 %collective-permute-start.5 = (f32[512,256]{1,0:T(8,128)S(1)}, f32[512,256]{1,0:T(8,128)S(1)}, u32[]{:S(2)}, u32[]{:S(2)}) collective-permute-start(f32[512,256]{1,0:T(8,128)S(1)} %slice.84), channel_id=1, source_target_pairs={{0,31},{1,0},{2,1},{3,2},{4,3},{5,4},{6,5},{7,6},{8,7},{9,8},{10,9... | collective-permute-start | bytes 1572872 | tf_op jit(solution)/shard_map/ppermute | solution.py:9
Sparse Core Ops, SparseCore 0:
  10.5 73.6 all-gather.4
  85.9 18.4 all-gather.6
  107.6 72.1 all-gather.8
  181.3 18.4 all-gather.10
where the time goes:
time: 250 us; the launch traced here: 249 us
  waiting for transfers between devices  179 us (72%)
  matrix products  26 us (10%)
  starting transfers between devices  19.7 us (8%)
  between operations  13.3 us (5%)
  local copies, waits for them, and re-layouts  10 us (4%)
    all_gather x1, waiting for transfers between devices, body(): rotations = lax.all_gather(left_rot, 'col', axis=1, tiled=True)  74.9 us
    all_gather x1, waiting for transfers between devices, body(): rotations = lax.all_gather(left_off, 'col', axis=1, tiled=True)  65.9 us
    ppermute x2, waiting for transfers between devices, padded_2(): lax.ppermute(tail, axis, [(i, (i + 1) % count) for i in range(count)])  17.1 us
    all_gather x1, waiting for transfers between devices, body(): rotations = lax.all_gather(right_rot, 'row', axis=1, tiled=True)  13.7 us
    ppermute x2, starting transfers between devices, passed_along(): return lax.ppermute(x, axis, [(i, (i + by) % size) for i in range(size)])  10.1 us
    dot_general x2, matrix products, apply_left(): jnp.einsum('kab,kac->kbc', rotations, shaped, precision=lax.Precision.HIG...  9.5 us
    ppermute x2, starting transfers between devices, padded_2(): lax.ppermute(head, axis, [((i + 1) % count, i) for i in range(count)])  8.95 us
    dot_general x1, matrix products, apply_right(): jnp.einsum('rka,kab->rkb', shaped, rotations, precision=lax.Precision.HIG...  5.33 us
  transfers between devices with their start and end apart: 10, of which 6 were waited for; matrix products, arithmetic and copies ran while one was open for 11% of the time, Pallas kernels for 0%

commit v1 on v0

v1 whole, which is shorter than its diff:
```python
import functools

import jax
import jax.numpy as jnp
from jax import lax
from jax.experimental import pallas as pl
from jax.experimental.pallas import tpu as pltpu
from jax.sharding import PartitionSpec as P

WIN = 512
HALF = 256
F32 = jnp.float32
BF16 = jnp.bfloat16


def xor_perm(axis, mask):
    return [(i, i ^ mask) for i in range(lax.axis_size(axis))]


def shift_perm(axis, by):
    size = lax.axis_size(axis)
    return [(i, (i + by) % size) for i in range(size)]


def swap(x, axis, mask):
    return lax.ppermute(x, axis, xor_perm(axis, mask))


def shift(x, axis, by):
    return lax.ppermute(x, axis, shift_perm(axis, by))


def split(x):
    hi = x.astype(BF16)
    lo = (x - hi.astype(F32)).astype(BF16)
    return hi, lo


def dot3(a, b, dims):
    dn = (dims, ((), ()))
    ah, al = a
    bh, bl = b
    dot = functools.partial(lax.dot_general, dimension_numbers=dn, preferred_element_type=F32)
    return dot(ah, bh) + (dot(ah, bl) + dot(al, bh))


NN = ((1,), (0,))
TN = ((0,), (0,))


def place_right(pieces, hi, lo):
    me = lax.axis_index("row")
    for k, piece in enumerate(pieces):
        rows = pl.ds(pl.multiple_of((me ^ k) * 128, 128), 128)
        h, l = split(piece[...])
        hi[rows, :] = h
        lo[rows, :] = l


def place_left(pieces, hi, lo):
    me = lax.axis_index("col")
    for kz, piece in enumerate(pieces):
        for j in range(4):
            for a in range(2):
                at = (me ^ (kz * 8 + a * 4 + j)) * 16
                rows = pl.ds(pl.multiple_of(at, 16), 16)
                h, l = split(piece[(j * 2 + a) * 16 : (j * 2 + a + 1) * 16, :])
                hi[rows, :] = h
                lo[rows, :] = l


def right_aligned(s, p0, p1, p2, p3, ml, mr, qh, ql):
    place_right((p0, p1, p2, p3), qh, ql)
    q = (qh[...], ql[...])
    m = dot3(split(s[...]), q, NN)
    ml[...] = m[:, :HALF]
    mr[...] = m[:, HALF:]


def right_shifted(ml, mr, hl, hr, p0, p1, p2, p3, out, qh, ql):
    place_right((p0, p1, p2, p3), qh, ql)
    for c, (u, v) in enumerate(((hl, ml), (mr, hr))):
        cols = slice(c * HALF, (c + 1) * HALF)
        top = (qh[:HALF, cols], ql[:HALF, cols])
        low = (qh[HALF:, cols], ql[HALF:, cols])
        out[:, cols] = dot3(split(u[...]), top, NN) + dot3(split(v[...]), low, NN)


def left_aligned(x, p0, p1, p2, p3, top, mid, low, qh, ql):
    place_left((p0, p1, p2, p3), qh, ql)
    for k in range(2):
        cols = slice(k * WIN, (k + 1) * WIN)
        n = dot3((qh[:, cols], ql[:, cols]), split(x[cols, :]), TN)
        if k == 0:
            top[...] = n[:HALF]
            mid[:HALF, :] = n[HALF:]
        else:
            mid[HALF:, :] = n[:HALF]
            low[...] = n[HALF:]


def left_shifted(top, mid, low, above, below, p0, p1, p2, p3, out, qh, ql):
    place_left((p0, p1, p2, p3), qh, ql)

    def q(rows, cols):
        return qh[rows, cols], ql[rows, cols]

    first, second = slice(0, HALF), slice(HALF, WIN)
    a, b, c = slice(0, HALF), slice(HALF, HALF + WIN), slice(HALF + WIN, 2 * WIN)
    out[a, :] = dot3(q(first, a), split(above[...]), TN) + dot3(q(second, a), split(top[...]), TN)
    out[b, :] = dot3(q(slice(None), b), split(mid[...]), TN)
    out[c, :] = dot3(q(first, c), split(low[...]), TN) + dot3(q(second, c), split(below[...]), TN)


def kernel_call(kernel, outs, scratch, flops, *args):
    bytes_moved = sum(4 * x.size for x in args) + sum(4 * a * b for a, b in outs)
    return pl.pallas_call(
        kernel,
        out_shape=tuple(jax.ShapeDtypeStruct(s, F32) for s in outs),
        in_specs=[pl.BlockSpec(memory_space=pltpu.VMEM)] * len(args),
        out_specs=tuple(pl.BlockSpec(memory_space=pltpu.VMEM) for _ in outs),
        scratch_shapes=[pltpu.VMEM(scratch, BF16), pltpu.VMEM(scratch, BF16)],
        compiler_params=pltpu.CompilerParams(vmem_limit_bytes=40 * 2**20),
        cost_estimate=pl.CostEstimate(flops=flops, bytes_accessed=bytes_moved, transcendentals=0),
    )(*args)


FLOPS = 3 * 2 * 1024 * 512 * 512


def gather_right(x):
    across = swap(x, "row", 2)
    core = swap(x, "row", 1)
    return x, core, across, swap(across, "row", 1)


def gather_left(x):
    x = jnp.concatenate([x, swap(x, "col", 4)], axis=0)
    x = jnp.concatenate([x] + [swap(x, "col", k) for k in (1, 2, 3)], axis=0)
    return [x] + [swap(x, "col", k * 8) for k in (1, 2, 3)]


def body(schur, left_rot, right_rot, left_off, right_off):
    r1 = gather_right(right_rot[0])
    l1 = gather_left(jnp.concatenate([left_rot[0], left_rot[1]], axis=1))
    ml, mr = kernel_call(right_aligned, [(1024, HALF)] * 2, (WIN, WIN), FLOPS, schur, *r1)
    hl = shift(mr, "col", 1)
    hr = shift(ml, "col", -1)
    following = shift(right_off[0][:, :HALF], "col", -1)
    r2 = gather_right(jnp.concatenate([right_off[0][:, HALF:], following], axis=1))
    following = shift(left_off[0][:, :HALF], "row", -1)
    l2 = gather_left(jnp.concatenate([left_off[0][:, HALF:], left_off[1], following], axis=1))
    (x,) = kernel_call(right_shifted, [(1024, WIN)], (WIN, WIN), FLOPS, ml, mr, hl, hr, *r2)
    top, mid, low = kernel_call(
        left_aligned, [(HALF, WIN), (WIN, WIN), (HALF, WIN)], (WIN, 2 * WIN), FLOPS, x, *l1
    )
    above = shift(low, "row", 1)
    below = shift(top, "row", -1)
    (out,) = kernel_call(
        left_shifted, [(1024, WIN)], (WIN, 2 * WIN), FLOPS, top, mid, low, above, below, *l2
    )
    return out


def solution(mesh):
    return jax.shard_map(
        body,
        mesh=mesh,
        in_specs=(
            P("row", "col"),
            P("row", "col", None),
            P("col", "row", None),
            P("row", "col", None),
            P("col", "row", None),
        ),
        out_specs=P("row", "col"),
        check_vma=False,
    )
```

time: 250 us -> 118 us (0.47)
  waiting for transfers between devices: 179 us -> 57.9 us
  matrix products: 26 us -> 0 us
  starting transfers between devices: 19.7 us -> 43 us
  between operations: 13.3 us -> 0.24 us
  Pallas kernels: 0 us -> 9.58 us
  local copies, waits for them, and re-layouts: 10 us -> 5.17 us
    all_gather x4 -> x0, waiting for transfers between devices: 155 us -> none  [the longest x1 74.9 us: body(): rotations = lax.all_gather(left_rot, 'col', axis=1, tiled=True)]
    ppermute x6 -> x26, waiting for transfers between devices: 21.4 us -> 57.9 us  [the longest x20 56.1 us: swap(): return lax.ppermute(x, axis, xor_perm(axis, mask))]
    dot_general x7 -> x0, matrix products: 26 us -> none  [the longest x2 9.5 us: apply_left(): jnp.einsum('kab,kac->kbc', rotations, shaped, precision=lax.Precision.HIG...]
    ppermute x6 -> x26, starting transfers between devices: 19.6 us -> 43 us  [the longest x20 24.6 us: swap(): return lax.ppermute(x, axis, xor_perm(axis, mask))]
    pallas_call x0 -> x4, Pallas kernels: none -> 9.58 us  [kernel_call(): pl.pallas_call(kernel, out_shape=tuple((jax.ShapeDtypeStruct(s, F32) for...]
    concatenate x1 -> x2, local copies, waits for them, and re-layouts: 2.88 us -> 0.02 us  [gather_left(): x = jnp.concatenate([x] + [swap(x, 'col', k) for k in (1, 2, 3)], axis=0)]
    slice x4 -> x2, local copies, waits for them, and re-layouts: 3.61 us -> 0.99 us  [the longest x1 0.99 us: body(): right_off[0][:, HALF:]]
    unnamed x4 -> x0, waiting for transfers between devices: 2.61 us -> none
  transfers between devices with their start and end apart: 10 -> 26, of which waited for: 6 -> 11; matrix products, arithmetic and copies ran while one was open for 11% -> 2% of each run, Pallas kernels for 0% -> 5%
where the time goes in v1:
time: 118 us; the launch traced here: 116 us
  waiting for transfers between devices  57.9 us (49%)
  starting transfers between devices  43 us (36%)
  Pallas kernels  9.58 us (8%)
  local copies, waits for them, and re-layouts  5.17 us (4%)
    ppermute x20, waiting for transfers between devices, swap(): return lax.ppermute(x, axis, xor_perm(axis, mask))  56.1 us
    ppermute x20, starting transfers between devices, swap(): return lax.ppermute(x, axis, xor_perm(axis, mask))  24.6 us
    ppermute x6, starting transfers between devices, shift(): return lax.ppermute(x, axis, shift_perm(axis, by))  18.5 us
    pallas_call x4, Pallas kernels, kernel_call(): pl.pallas_call(kernel, out_shape=tuple((jax.ShapeDtypeStruct(s, F32) for...  9.58 us
    unnamed x10, local copies, waits for them, and re-layouts  2.59 us
  transfers between devices with their start and end apart: 26, of which 11 were waited for; matrix products, arithmetic and copies ran while one was open for 2% of the time, Pallas kernels for 5%

profile of v1, /device:TPU:0, one launch (start us, length us, event | category | flops | bytes accessed | tf_op | source)
XLA Modules:
  0.0 116.0 jit_solution(7203181081306749020)
XLA Ops:
  0.0 1.6 %collective-permute-start.1 = (f32[128,512]{1,0:T(8,128)}, f32[128,512]{1,0:T(8,128)S(1)}, u32[]{:S(2)}, u32[]{:S(2)}) collective-permute-start(f32[128,512]{1,0:T(8,128)} %bitcast.10), channel_id=1, source_target_pairs={{0,64},{32,96},{64,0},{96,32},{1,65},{33,97},{65,1},{97,33},{2,66}... | collective-permute-start | bytes 786440 | tf_op jit(solution)/shard_map/ppermute | solution.py:26
  1.6 1.0 fusion
  2.6 8.7 %collective-permute-start.5 = (f32[128,256]{1,0:T(8,128)S(1)}, f32[128,256]{1,0:T(8,128)S(1)}, u32[]{:S(2)}, u32[]{:S(2)}) collective-permute-start(f32[128,256]{1,0:T(8,128)S(1)} %get-tuple-element.16), channel_id=1, source_target_pairs={{0,31},{1,0},{2,1},{3,2},{4,3},{5,4},{6,5},{7,6},{8,7},{9,8},{10,9... | collective-permute-start | bytes 393224 | tf_op jit(solution)/shard_map/ppermute | solution.py:30
  11.3 0.8 slice_bitcast_fusion
  12.2 0.8 slice_bitcast_fusion.3
  13.6 1.8 %collective-permute-done.18 = f32[16,256]{1,0:T(8,128)S(1)} collective-permute-done((f32[16,256]{1,0:T(8,128)S(1)}, f32[16,256]{1,0:T(8,128)S(1)}, u32[]{:S(2)}, u32[]{:S(2)}) %collective-permute-start.18) | collective-permute-done | bytes 16416 | tf_op jit(solution)/shard_map/ppermute | solution.py:30
  15.5 1.4 %collective-permute-start.19 = (f32[16,1024]{1,0:T(8,128)S(1)}, f32[16,1024]{1,0:T(8,128)S(1)}, u32[]{:S(2)}, u32[]{:S(2)}) collective-permute-start(f32[16,1024]{1,0:T(8,128)S(1)} %get-tuple-element.17), channel_id=1, source_target_pairs={{0,4},{1,5},{2,6},{3,7},{4,0},{5,1},{6,2},{7,3},{8,12},{9,13},{10,... | collective-permute-start | bytes 196616 | tf_op jit(solution)/shard_map/ppermute | solution.py:26
  16.9 2.2 %collective-permute-done.9 = f32[16,1024]{1,0:T(8,128)S(1)} collective-permute-done((f32[16,1024]{1,0:T(8,128)S(1)}, f32[16,1024]{1,0:T(8,128)S(1)}, u32[]{:S(2)}, u32[]{:S(2)}) %collective-permute-start.9) | collective-permute-done | bytes 65568 | tf_op jit(solution)/shard_map/ppermute | solution.py:26
  19.3 4.7 %collective-permute-start.12 = (f32[32,1024]{1,0:T(8,128)S(1)}, f32[32,1024]{1,0:T(8,128)S(1)}, u32[]{:S(2)}, u32[]{:S(2)}) collective-permute-start(f32[32,1024]{1,0:T(8,128)S(1)} %pad_maximum_fusion.1), channel_id=1, source_target_pairs={{0,3},{1,2},{2,1},{3,0},{4,7},{5,6},{6,5},{7,4},{8,11},{9,10},{10,... | collective-permute-start | bytes 393224 | tf_op jit(solution)/shard_map/ppermute | solution.py:26
  23.9 1.6 %collective-permute-start.7 = (f32[128,512]{1,0:T(8,128)S(1)}, f32[128,512]{1,0:T(8,128)S(1)}, u32[]{:S(2)}, u32[]{:S(2)}) collective-permute-start(f32[128,512]{1,0:T(8,128)S(1)} %pad_maximum_fusion.p0), channel_id=1, source_target_pairs={{0,64},{32,96},{64,0},{96,32},{1,65},{33,97},{65,1},{97,33},{2,66}... | collective-permute-start | bytes 786440 | tf_op jit(solution)/shard_map/ppermute | solution.py:26
  25.6 1.6 %copy-done = f32[1024,512]{1,0:T(8,128)S(1)} copy-done((f32[1024,512]{1,0:T(8,128)S(1)}, f32[1024,512]{1,0:T(8,128)}, u32[]{:S(2)}) %copy-start) | copy-done | bytes 2097176
  27.2 0.9 copy-done.1
  28.1 2.0 %shard_map.55 = (f32[1024,256]{1,0:T(8,128)S(1)}, f32[1024,256]{1,0:T(8,128)S(1)}) custom-call(f32[1024,512]{1,0:T(8,128)S(1)} %copy-done, f32[128,512]{1,0:T(8,128)S(1)} %bitcast.12, f32[128,512]{1,0:T(8,128)S(1)} %collective-permute-done.p1, f32[128,512]{1,0:T(8,128)S(1)} %collective-permute-done.1.p2, f32[128,512]{1,0:T(8,128)S(1)} %collective-permute-done.2.p3), custom_call_target="tpu_custom_call" | custom-call | flops 1610612736 | bytes 5242880 | tf_op jit(solution)/shard_map/pallas_call | solution.py:117
  30.2 7.7 %collective-permute-start.4 = (f32[1024,256]{1,0:T(8,128)S(1)}, f32[1024,256]{1,0:T(8,128)S(1)}, u32[]{:S(2)}, u32[]{:S(2)}) collective-permute-start(f32[1024,256]{1,0:T(8,128)S(1)} %get-tuple-element.10.ml), channel_id=1, source_target_pairs={{0,31},{1,0},{2,1},{3,2},{4,3},{5,4},{6,5},{7,6},{8,7},{9,8},{10,9... | collective-permute-start | bytes 3145736 | tf_op jit(solution)/shard_map/ppermute | solution.py:30
  38.2 18.6 %collective-permute-done.20 = f32[32,1024]{1,0:T(8,128)S(1)} collective-permute-done((f32[32,1024]{1,0:T(8,128)S(1)}, f32[32,1024]{1,0:T(8,128)S(1)}, u32[]{:S(2)}, u32[]{:S(2)}) %collective-permute-start.20) | collective-permute-done | bytes 131104 | tf_op jit(solution)/shard_map/ppermute | solution.py:26
  57.3 0.6 collective-permute-done.21
  57.9 5.3 %collective-permute-start.22 = (f32[32,1024]{1,0:T(8,128)S(1)}, f32[32,1024]{1,0:T(8,128)S(1)}, u32[]{:S(2)}, u32[]{:S(2)}) collective-permute-start(f32[32,1024]{1,0:T(8,128)S(1)} %pad_maximum_fusion.2), channel_id=1, source_target_pairs={{0,3},{1,2},{2,1},{3,0},{4,7},{5,6},{6,5},{7,4},{8,11},{9,10},{10,... | collective-permute-start | bytes 393224 | tf_op jit(solution)/shard_map/ppermute | solution.py:26
  63.2 2.9 %collective-permute-done.22 = f32[32,1024]{1,0:T(8,128)S(1)} collective-permute-done((f32[32,1024]{1,0:T(8,128)S(1)}, f32[32,1024]{1,0:T(8,128)S(1)}, u32[]{:S(2)}, u32[]{:S(2)}) %collective-permute-start.22) | collective-permute-done | bytes 131104 | tf_op jit(solution)/shard_map/ppermute | solution.py:26
  66.1 2.6 %collective-permute-start.14 = (f32[128,1024]{1,0:T(8,128)S(1)}, f32[128,1024]{1,0:T(8,128)S(1)}, u32[]{:S(2)}, u32[]{:S(2)}) collective-permute-start(f32[128,1024]{1,0:T(8,128)S(1)} %constant_dynamic-update-slice_fusion.p0), channel_id=1, source_target_pairs={{0,16},{1,17},{2,18},{3,19},{4,20},{5,21},{6,22},{7,23},{8,24},{9,... | collective-permute-start | bytes 1572872 | tf_op jit(solution)/shard_map/ppermute | solution.py:26
  68.8 2.1 %collective-permute-start.15 = (f32[128,1024]{1,0:T(8,128)S(1)}, f32[128,1024]{1,0:T(8,128)S(1)}, u32[]{:S(2)}, u32[]{:S(2)}) collective-permute-start(f32[128,1024]{1,0:T(8,128)S(1)} %constant_dynamic-update-slice_fusion.p0), channel_id=1, source_target_pairs={{0,24},{1,25},{2,26},{3,27},{4,28},{5,29},{6,30},{7,31},{8,16},{9,... | collective-permute-start | bytes 1572872 | tf_op jit(solution)/shard_map/ppermute | solution.py:26
  71.0 2.6 %collective-permute-start.24 = (f32[128,1024]{1,0:T(8,128)S(1)}, f32[128,1024]{1,0:T(8,128)S(1)}, u32[]{:S(2)}, u32[]{:S(2)}) collective-permute-start(f32[128,1024]{1,0:T(8,128)S(1)} %constant_dynamic-update-slice_fusion.5.p0), channel_id=1, source_target_pairs={{0,16},{1,17},{2,18},{3,19},{4,20},{5,21},{6,22},{7,23},{8,24},{9,... | collective-permute-start | bytes 1572872 | tf_op jit(solution)/shard_map/ppermute | solution.py:26
  73.6 2.0 %shard_map.56.x = f32[1024,512]{1,0:T(8,128)S(1)} custom-call(f32[1024,256]{1,0:T(8,128)S(1)} %get-tuple-element.10.ml, f32[1024,256]{1,0:T(8,128)S(1)} %get-tuple-element.11.mr, f32[1024,256]{1,0:T(8,128)S(1)} %collective-permute-done.3.hl, f32[1024,256]{1,0:T(8,128)S(1)} %collective-permute-done.4.hr, f32[128,512]{1,0:T(8,128)S(1)} %pad_maximum_fusion.p0, ...), custom_call_target="tpu_custom_call" | custom-call | flops 1610612736 | bytes 7340032 | tf_op jit(solution)/shard_map/pallas_call | solution.py:117
  75.6 5.4 %collective-permute-done.13.p1 = f32[128,1024]{1,0:T(8,128)S(1)} collective-permute-done((f32[128,1024]{1,0:T(8,128)S(1)}, f32[128,1024]{1,0:T(8,128)S(1)}, u32[]{:S(2)}, u32[]{:S(2)}) %collective-permute-start.13) | collective-permute-done | bytes 524320 | tf_op jit(solution)/shard_map/ppermute | solution.py:26
  81.0 1.2 collective-permute-start.25
  82.1 10.7 %collective-permute-done.14.p2 = f32[128,1024]{1,0:T(8,128)S(1)} collective-permute-done((f32[128,1024]{1,0:T(8,128)S(1)}, f32[128,1024]{1,0:T(8,128)S(1)}, u32[]{:S(2)}, u32[]{:S(2)}) %collective-permute-start.14) | collective-permute-done | bytes 524320 | tf_op jit(solution)/shard_map/ppermute | solution.py:26
  92.8 3.3 %collective-permute-done.15.p3 = f32[128,1024]{1,0:T(8,128)S(1)} collective-permute-done((f32[128,1024]{1,0:T(8,128)S(1)}, f32[128,1024]{1,0:T(8,128)S(1)}, u32[]{:S(2)}, u32[]{:S(2)}) %collective-permute-start.15) | collective-permute-done | bytes 524320 | tf_op jit(solution)/shard_map/ppermute | solution.py:26
  96.1 2.1 %shard_map.57 = (f32[256,512]{1,0:T(8,128)S(1)}, f32[512,512]{1,0:T(8,128)S(1)}, f32[256,512]{1,0:T(8,128)S(1)}) custom-call(f32[1024,512]{1,0:T(8,128)S(1)} %shard_map.56.x, f32[128,1024]{1,0:T(8,128)S(1)} %constant_dynamic-update-slice_fusion.p0, f32[128,1024]{1,0:T(8,128)S(1)} %collective-permute-done.13.p1, f32[128,1024]{1,0:T(8,128)S(1)} %collective-permute-done.14.p2, ...), custom_call_target="tpu_custom_call" | custom-call | flops 1610612736 | bytes 6291456 | tf_op jit(solution)/shard_map/pallas_call | solution.py:117
  98.3 1.7 %collective-permute-start.17 = (f32[256,512]{1,0:T(8,128)S(1)}, f32[256,512]{1,0:T(8,128)S(1)}, u32[]{:S(2)}, u32[]{:S(2)}) collective-permute-start(f32[256,512]{1,0:T(8,128)S(1)} %get-tuple-element.12.top), channel_id=1, source_target_pairs={{0,96},{32,0},{64,32},{96,64},{1,97},{33,1},{65,33},{97,65},{2,98}... | collective-permute-start | bytes 1572872 | tf_op jit(solution)/shard_map/ppermute | solution.py:30
  100.1 3.4 %collective-permute-done.23.p1 = f32[128,1024]{1,0:T(8,128)S(1)} collective-permute-done((f32[128,1024]{1,0:T(8,128)S(1)}, f32[128,1024]{1,0:T(8,128)S(1)}, u32[]{:S(2)}, u32[]{:S(2)}) %collective-permute-start.23) | collective-permute-done | bytes 524320 | tf_op jit(solution)/shard_map/ppermute | solution.py:26
  103.5 6.4 %collective-permute-done.24.p2 = f32[128,1024]{1,0:T(8,128)S(1)} collective-permute-done((f32[128,1024]{1,0:T(8,128)S(1)}, f32[128,1024]{1,0:T(8,128)S(1)}, u32[]{:S(2)}, u32[]{:S(2)}) %collective-permute-start.24) | collective-permute-done | bytes 524320 | tf_op jit(solution)/shard_map/ppermute | solution.py:26
  109.9 2.6 %collective-permute-done.25.p3 = f32[128,1024]{1,0:T(8,128)S(1)} collective-permute-done((f32[128,1024]{1,0:T(8,128)S(1)}, f32[128,1024]{1,0:T(8,128)S(1)}, u32[]{:S(2)}, u32[]{:S(2)}) %collective-permute-start.25) | collective-permute-done | bytes 524320 | tf_op jit(solution)/shard_map/ppermute | solution.py:26
  112.5 3.5 %shard_map.58 = f32[1024,512]{1,0:T(8,128)} custom-call(f32[256,512]{1,0:T(8,128)S(1)} %get-tuple-element.12.top, f32[512,512]{1,0:T(8,128)S(1)} %get-tuple-element.13.mid, f32[256,512]{1,0:T(8,128)S(1)} %get-tuple-element.14.low, f32[256,512]{1,0:T(8,128)S(1)} %collective-permute-done.16.above, f32[256,512]{1,0:T(8,128)S(1)} %collective-permute-done.17.below, ...), custom_call_target="tpu_custom_call" | custom-call | flops 1610612736 | bytes 7340032 | tf_op jit(solution)/shard_map/pallas_call | solution.py:117
  (45 shorter events, 2.0 us)
Async XLA Ops:
  0.0 13.1 %collective-permute-start.1 = (f32[128,512]{1,0:T(8,128)}, f32[128,512]{1,0:T(8,128)S(1)}, u32[]{:S(2)}, u32[]{:S(2)}) collective-permute-start(f32[128,512]{1,0:T(8,128)} %bitcast.10), channel_id=1, source_target_pairs={{0,64},{32,96},{64,0},{96,32},{1,65},{33,97},{65,1},{97,33},{2,66}... | collective-permute-start | bytes 786440 | tf_op jit(solution)/shard_map/ppermute | solution.py:26
  1.6 17.7 %collective-permute-start = (f32[128,512]{1,0:T(8,128)}, f32[128,512]{1,0:T(8,128)S(1)}, u32[]{:S(2)}, u32[]{:S(2)}) collective-permute-start(f32[128,512]{1,0:T(8,128)} %bitcast.11), channel_id=1, source_target_pairs={{0,32},{32,0},{64,96},{96,64},{1,33},{33,1},{65,97},{97,65},{2,34}... | collective-permute-start | bytes 786440 | tf_op jit(solution)/shard_map/ppermute | solution.py:26
  2.6 16.6 %collective-permute-start.5 = (f32[128,256]{1,0:T(8,128)S(1)}, f32[128,256]{1,0:T(8,128)S(1)}, u32[]{:S(2)}, u32[]{:S(2)}) collective-permute-start(f32[128,256]{1,0:T(8,128)S(1)} %get-tuple-element.16), channel_id=1, source_target_pairs={{0,31},{1,0},{2,1},{3,2},{4,3},{5,4},{6,5},{7,6},{8,7},{9,8},{10,9... | collective-permute-start | bytes 393224 | tf_op jit(solution)/shard_map/ppermute | solution.py:30
  12.1 3.4 %collective-permute-start.18 = (f32[16,256]{1,0:T(8,128)S(1)}, f32[16,256]{1,0:T(8,128)S(1)}, u32[]{:S(2)}, u32[]{:S(2)}) collective-permute-start(f32[16,256]{1,0:T(8,128)S(1)} %get-tuple-element.26), channel_id=1, source_target_pairs={{0,96},{32,0},{64,32},{96,64},{1,97},{33,1},{65,33},{97,65},{2,98}... | collective-permute-start | bytes 49160 | tf_op jit(solution)/shard_map/ppermute | solution.py:30
  13.0 6.0 %collective-permute-start.9 = (f32[16,1024]{1,0:T(8,128)S(1)}, f32[16,1024]{1,0:T(8,128)S(1)}, u32[]{:S(2)}, u32[]{:S(2)}) collective-permute-start(f32[16,1024]{1,0:T(8,128)S(1)} %get-tuple-element.21), channel_id=1, source_target_pairs={{0,4},{1,5},{2,6},{3,7},{4,0},{5,1},{6,2},{7,3},{8,12},{9,13},{10,... | collective-permute-start | bytes 196616 | tf_op jit(solution)/shard_map/ppermute | solution.py:26
  13.1 10.8 %collective-permute-start.2 = (f32[128,512]{1,0:T(8,128)S(1)}, f32[128,512]{1,0:T(8,128)S(1)}, u32[]{:S(2)}, u32[]{:S(2)}) collective-permute-start(f32[128,512]{1,0:T(8,128)S(1)} %collective-permute-done.1.p2), channel_id=1, source_target_pairs={{0,32},{32,0},{64,96},{96,64},{1,33},{33,1},{65,97},{97,65},{2,34}... | collective-permute-start | bytes 786440 | tf_op jit(solution)/shard_map/ppermute | solution.py:26
  15.5 14.6 %collective-permute-start.19 = (f32[16,1024]{1,0:T(8,128)S(1)}, f32[16,1024]{1,0:T(8,128)S(1)}, u32[]{:S(2)}, u32[]{:S(2)}) collective-permute-start(f32[16,1024]{1,0:T(8,128)S(1)} %get-tuple-element.17), channel_id=1, source_target_pairs={{0,4},{1,5},{2,6},{3,7},{4,0},{5,1},{6,2},{7,3},{8,12},{9,13},{10,... | collective-permute-start | bytes 196616 | tf_op jit(solution)/shard_map/ppermute | solution.py:26
  19.0 11.2 %collective-permute-start.10 = (f32[32,1024]{1,0:T(8,128)S(1)}, f32[32,1024]{1,0:T(8,128)S(1)}, u32[]{:S(2)}, u32[]{:S(2)}) collective-permute-start(f32[32,1024]{1,0:T(8,128)S(1)} %pad_maximum_fusion.1), channel_id=1, source_target_pairs={{0,1},{1,0},{2,3},{3,2},{4,5},{5,4},{6,7},{7,6},{8,9},{9,8},{10,11... | collective-permute-start | bytes 393224 | tf_op jit(solution)/shard_map/ppermute | solution.py:26
  19.1 18.8 %collective-permute-start.11 = (f32[32,1024]{1,0:T(8,128)S(1)}, f32[32,1024]{1,0:T(8,128)S(1)}, u32[]{:S(2)}, u32[]{:S(2)}) collective-permute-start(f32[32,1024]{1,0:T(8,128)S(1)} %pad_maximum_fusion.1), channel_id=1, source_target_pairs={{0,2},{1,3},{2,0},{3,1},{4,6},{5,7},{6,4},{7,5},{8,10},{9,11},{10,... | collective-permute-start | bytes 393224 | tf_op jit(solution)/shard_map/ppermute | solution.py:26
  19.3 18.8 %collective-permute-start.12 = (f32[32,1024]{1,0:T(8,128)S(1)}, f32[32,1024]{1,0:T(8,128)S(1)}, u32[]{:S(2)}, u32[]{:S(2)}) collective-permute-start(f32[32,1024]{1,0:T(8,128)S(1)} %pad_maximum_fusion.1), channel_id=1, source_target_pairs={{0,3},{1,2},{2,1},{3,0},{4,7},{5,6},{6,5},{7,4},{8,11},{9,10},{10,... | collective-permute-start | bytes 393224 | tf_op jit(solution)/shard_map/ppermute | solution.py:26
  23.9 32.8 %collective-permute-start.7 = (f32[128,512]{1,0:T(8,128)S(1)}, f32[128,512]{1,0:T(8,128)S(1)}, u32[]{:S(2)}, u32[]{:S(2)}) collective-permute-start(f32[128,512]{1,0:T(8,128)S(1)} %pad_maximum_fusion.p0), channel_id=1, source_target_pairs={{0,64},{32,96},{64,0},{96,32},{1,65},{33,97},{65,1},{97,33},{2,66}... | collective-permute-start | bytes 786440 | tf_op jit(solution)/shard_map/ppermute | solution.py:26
  25.6 1.6 %copy-start = (f32[1024,512]{1,0:T(8,128)S(1)}, f32[1024,512]{1,0:T(8,128)}, u32[]{:S(2)}) copy-start(f32[1024,512]{1,0:T(8,128)} %s.1) | copy-start | bytes 6291460
  27.2 0.9 copy-start.1
  30.1 40.8 %collective-permute-start.3 = (f32[1024,256]{1,0:T(8,128)S(1)}, f32[1024,256]{1,0:T(8,128)S(1)}, u32[]{:S(2)}, u32[]{:S(2)}) collective-permute-start(f32[1024,256]{1,0:T(8,128)S(1)} %get-tuple-element.11.mr), channel_id=1, source_target_pairs={{0,1},{1,2},{2,3},{3,4},{4,5},{5,6},{6,7},{7,8},{8,9},{9,10},{10,1... | collective-permute-start | bytes 3145736 | tf_op jit(solution)/shard_map/ppermute | solution.py:30
  30.2 40.8 %collective-permute-start.4 = (f32[1024,256]{1,0:T(8,128)S(1)}, f32[1024,256]{1,0:T(8,128)S(1)}, u32[]{:S(2)}, u32[]{:S(2)}) collective-permute-start(f32[1024,256]{1,0:T(8,128)S(1)} %get-tuple-element.10.ml), channel_id=1, source_target_pairs={{0,31},{1,0},{2,1},{3,2},{4,3},{5,4},{6,5},{7,6},{8,7},{9,8},{10,9... | collective-permute-start | bytes 3145736 | tf_op jit(solution)/shard_map/ppermute | solution.py:30
  38.0 18.8 %collective-permute-start.20 = (f32[32,1024]{1,0:T(8,128)S(1)}, f32[32,1024]{1,0:T(8,128)S(1)}, u32[]{:S(2)}, u32[]{:S(2)}) collective-permute-start(f32[32,1024]{1,0:T(8,128)S(1)} %pad_maximum_fusion.2), channel_id=1, source_target_pairs={{0,1},{1,0},{2,3},{3,2},{4,5},{5,4},{6,7},{7,6},{8,9},{9,8},{10,11... | collective-permute-start | bytes 393224 | tf_op jit(solution)/shard_map/ppermute | solution.py:26
  38.1 19.8 %collective-permute-start.21 = (f32[32,1024]{1,0:T(8,128)S(1)}, f32[32,1024]{1,0:T(8,128)S(1)}, u32[]{:S(2)}, u32[]{:S(2)}) collective-permute-start(f32[32,1024]{1,0:T(8,128)S(1)} %pad_maximum_fusion.2), channel_id=1, source_target_pairs={{0,2},{1,3},{2,0},{3,1},{4,6},{5,7},{6,4},{7,5},{8,10},{9,11},{10,... | collective-permute-start | bytes 393224 | tf_op jit(solution)/shard_map/ppermute | solution.py:26
  56.8 9.4 %collective-permute-start.6 = (f32[128,512]{1,0:T(8,128)S(1)}, f32[128,512]{1,0:T(8,128)S(1)}, u32[]{:S(2)}, u32[]{:S(2)}) collective-permute-start(f32[128,512]{1,0:T(8,128)S(1)} %pad_maximum_fusion.p0), channel_id=1, source_target_pairs={{0,32},{32,0},{64,96},{96,64},{1,33},{33,1},{65,97},{97,65},{2,34}... | collective-permute-start | bytes 786440 | tf_op jit(solution)/shard_map/ppermute | solution.py:26
  56.8 12.0 %collective-permute-start.8 = (f32[128,512]{1,0:T(8,128)S(1)}, f32[128,512]{1,0:T(8,128)S(1)}, u32[]{:S(2)}, u32[]{:S(2)}) collective-permute-start(f32[128,512]{1,0:T(8,128)S(1)} %collective-permute-done.7.p2), channel_id=1, source_target_pairs={{0,32},{32,0},{64,96},{96,64},{1,33},{33,1},{65,97},{97,65},{2,34}... | collective-permute-start | bytes 786440 | tf_op jit(solution)/shard_map/ppermute | solution.py:26
  57.9 8.2 %collective-permute-start.22 = (f32[32,1024]{1,0:T(8,128)S(1)}, f32[32,1024]{1,0:T(8,128)S(1)}, u32[]{:S(2)}, u32[]{:S(2)}) collective-permute-start(f32[32,1024]{1,0:T(8,128)S(1)} %pad_maximum_fusion.2), channel_id=1, source_target_pairs={{0,3},{1,2},{2,1},{3,0},{4,7},{5,6},{6,5},{7,4},{8,11},{9,10},{10,... | collective-permute-start | bytes 393224 | tf_op jit(solution)/shard_map/ppermute | solution.py:26
  66.1 14.9 %collective-permute-start.13 = (f32[128,1024]{1,0:T(8,128)S(1)}, f32[128,1024]{1,0:T(8,128)S(1)}, u32[]{:S(2)}, u32[]{:S(2)}) collective-permute-start(f32[128,1024]{1,0:T(8,128)S(1)} %constant_dynamic-update-slice_fusion.p0), channel_id=1, source_target_pairs={{0,8},{1,9},{2,10},{3,11},{4,12},{5,13},{6,14},{7,15},{8,0},{9,1},... | collective-permute-start | bytes 1572872 | tf_op jit(solution)/shard_map/ppermute | solution.py:26
  66.1 26.7 %collective-permute-start.14 = (f32[128,1024]{1,0:T(8,128)S(1)}, f32[128,1024]{1,0:T(8,128)S(1)}, u32[]{:S(2)}, u32[]{:S(2)}) collective-permute-start(f32[128,1024]{1,0:T(8,128)S(1)} %constant_dynamic-update-slice_fusion.p0), channel_id=1, source_target_pairs={{0,16},{1,17},{2,18},{3,19},{4,20},{5,21},{6,22},{7,23},{8,24},{9,... | collective-permute-start | bytes 1572872 | tf_op jit(solution)/shard_map/ppermute | solution.py:26
  68.8 27.4 %collective-permute-start.15 = (f32[128,1024]{1,0:T(8,128)S(1)}, f32[128,1024]{1,0:T(8,128)S(1)}, u32[]{:S(2)}, u32[]{:S(2)}) collective-permute-start(f32[128,1024]{1,0:T(8,128)S(1)} %constant_dynamic-update-slice_fusion.p0), channel_id=1, source_target_pairs={{0,24},{1,25},{2,26},{3,27},{4,28},{5,29},{6,30},{7,31},{8,16},{9,... | collective-permute-start | bytes 1572872 | tf_op jit(solution)/shard_map/ppermute | solution.py:26
  70.9 32.6 %collective-permute-start.23 = (f32[128,1024]{1,0:T(8,128)S(1)}, f32[128,1024]{1,0:T(8,128)S(1)}, u32[]{:S(2)}, u32[]{:S(2)}) collective-permute-start(f32[128,1024]{1,0:T(8,128)S(1)} %constant_dynamic-update-slice_fusion.5.p0), channel_id=1, source_target_pairs={{0,8},{1,9},{2,10},{3,11},{4,12},{5,13},{6,14},{7,15},{8,0},{9,1},... | collective-permute-start | bytes 1572872 | tf_op jit(solution)/shard_map/ppermute | solution.py:26
  71.0 38.9 %collective-permute-start.24 = (f32[128,1024]{1,0:T(8,128)S(1)}, f32[128,1024]{1,0:T(8,128)S(1)}, u32[]{:S(2)}, u32[]{:S(2)}) collective-permute-start(f32[128,1024]{1,0:T(8,128)S(1)} %constant_dynamic-update-slice_fusion.5.p0), channel_id=1, source_target_pairs={{0,16},{1,17},{2,18},{3,19},{4,20},{5,21},{6,22},{7,23},{8,24},{9,... | collective-permute-start | bytes 1572872 | tf_op jit(solution)/shard_map/ppermute | solution.py:26
  81.0 31.5 %collective-permute-start.25 = (f32[128,1024]{1,0:T(8,128)S(1)}, f32[128,1024]{1,0:T(8,128)S(1)}, u32[]{:S(2)}, u32[]{:S(2)}) collective-permute-start(f32[128,1024]{1,0:T(8,128)S(1)} %constant_dynamic-update-slice_fusion.5.p0), channel_id=1, source_target_pairs={{0,24},{1,25},{2,26},{3,27},{4,28},{5,29},{6,30},{7,31},{8,16},{9,... | collective-permute-start | bytes 1572872 | tf_op jit(solution)/shard_map/ppermute | solution.py:26
  98.3 14.2 %collective-permute-start.16 = (f32[256,512]{1,0:T(8,128)S(1)}, f32[256,512]{1,0:T(8,128)S(1)}, u32[]{:S(2)}, u32[]{:S(2)}) collective-permute-start(f32[256,512]{1,0:T(8,128)S(1)} %get-tuple-element.14.low), channel_id=1, source_target_pairs={{0,32},{32,64},{64,96},{96,0},{1,33},{33,65},{65,97},{97,1},{2,34}... | collective-permute-start | bytes 1572872 | tf_op jit(solution)/shard_map/ppermute | solution.py:30
  98.3 14.1 %collective-permute-start.17 = (f32[256,512]{1,0:T(8,128)S(1)}, f32[256,512]{1,0:T(8,128)S(1)}, u32[]{:S(2)}, u32[]{:S(2)}) collective-permute-start(f32[256,512]{1,0:T(8,128)S(1)} %get-tuple-element.12.top), channel_id=1, source_target_pairs={{0,96},{32,0},{64,32},{96,64},{1,97},{33,1},{65,33},{97,65},{2,98}... | collective-permute-start | bytes 1572872 | tf_op jit(solution)/shard_map/ppermute | solution.py:30

commit v2 on v1

v2 whole, which is shorter than its diff:
```python
import functools

import jax
import jax.numpy as jnp
from jax import lax
from jax.experimental import pallas as pl
from jax.experimental.pallas import tpu as pltpu
from jax.sharding import PartitionSpec as P

WIN = 512
HALF = 256
F32 = jnp.float32
BF16 = jnp.bfloat16


def xor_perm(axis, mask):
    return [(i, i ^ mask) for i in range(lax.axis_size(axis))]


def shift_perm(axis, by):
    size = lax.axis_size(axis)
    return [(i, (i + by) % size) for i in range(size)]


def swap(x, axis, mask):
    return lax.ppermute(x, axis, xor_perm(axis, mask))


def shift(x, axis, by):
    return lax.ppermute(x, axis, shift_perm(axis, by))


def split(x):
    hi = x.astype(BF16)
    lo = (x - hi.astype(F32)).astype(BF16)
    return hi, lo


def dot3(a, b, dims):
    dn = (dims, ((), ()))
    ah, al = a
    bh, bl = b
    dot = functools.partial(lax.dot_general, dimension_numbers=dn, preferred_element_type=F32)
    return dot(ah, bh) + (dot(ah, bl) + dot(al, bh))


NN = ((1,), (0,))
TN = ((0,), (0,))


def place_right(own, core, cols, place, hi, lo):
    me = lax.axis_index("row")
    for mask, source, at in ((0, own, 0), (2, own, 128), (1, core, 0), (3, core, 128)):
        rows = pl.ds(pl.multiple_of((me ^ mask) * 128, 128), 128)
        h, l = split(source[at : at + 128, cols])
        hi[rows, place] = h
        lo[rows, place] = l


def place_left(pieces, hi, lo):
    z = lax.axis_index("col") // 8
    own, up, down, far_first, far_second = pieces
    for by, at, source in ((0, 0, own), (3, 0, up), (1, 0, down), (2, 0, far_first), (2, 64, far_second)):
        size = source.shape[0]
        rows = pl.ds(pl.multiple_of((z + by) % 4 * 128 + at, size), size)
        h, l = split(source[...])
        hi[rows, :] = h
        lo[rows, :] = l


def right_aligned(s, own, core, *rest):
    ml, mr, rows, qh, ql, sems = rest[-6:]
    tile = rows.shape[0] // sems.shape[0]
    tiles = [slice(k * tile, (k + 1) * tile) for k in range(sems.shape[0])]
    reads = [pltpu.make_async_copy(s.at[t], rows.at[t], sems.at[k]) for k, t in enumerate(tiles)]
    for read in reads:
        read.start()
    place_right(own, core, slice(0, WIN), slice(0, WIN), qh, ql)
    for t, read in zip(tiles, reads):
        read.wait()
        m = dot3(split(rows[t, :]), (qh[...], ql[...]), NN)
        ml[t, :] = m[:, :HALF]
        mr[t, :] = m[:, HALF:]


def middle(ml, mr, hl, hr, own, core, next_own, next_core, p0, p1, p2, p3, p4, *rest):
    top, mid, low, x, qh, ql, lh, ll = rest[-8:]
    place_right(own, core, slice(WIN, WIN + HALF), slice(0, HALF), qh, ql)
    place_right(next_own, next_core, slice(0, HALF), slice(HALF, WIN), qh, ql)
    for c, (u, v) in enumerate(((hl, ml), (mr, hr))):
        cols = slice(c * HALF, (c + 1) * HALF)
        first = (qh[:HALF, cols], ql[:HALF, cols])
        second = (qh[HALF:, cols], ql[HALF:, cols])
        x[:, cols] = dot3(split(u[...]), first, NN) + dot3(split(v[...]), second, NN)
    place_left((p0, p1, p2, p3, p4), lh, ll)
    for k in range(2):
        cols = slice(k * WIN, (k + 1) * WIN)
        n = dot3((lh[:, cols], ll[:, cols]), split(x[cols, :]), TN)
        if k == 0:
            top[...] = n[:HALF]
            mid[:HALF, :] = n[HALF:]
        else:
            mid[HALF:, :] = n[:HALF]
            low[...] = n[HALF:]


def left_shifted(top, mid, low, above, below, p0, p1, p2, p3, p4, out, y, qh, ql, sems):
    place_left((p0, p1, p2, p3, p4), qh, ql)

    def q(rows, cols):
        return qh[rows, cols], ql[rows, cols]

    def write(part, k):
        copy = pltpu.make_async_copy(y.at[part], out.at[part], sems.at[k])
        copy.start()
        return copy

    first, second = slice(0, HALF), slice(HALF, WIN)
    a, b, c = slice(0, HALF), slice(HALF, HALF + WIN), slice(HALF + WIN, 2 * WIN)
    y[b, :] = dot3(q(slice(None), b), split(mid[...]), TN)
    writes = [write(b, 0)]
    y[a, :] = dot3(q(first, a), split(above[...]), TN) + dot3(q(second, a), split(top[...]), TN)
    writes.append(write(a, 1))
    y[c, :] = dot3(q(first, c), split(low[...]), TN) + dot3(q(second, c), split(below[...]), TN)
    writes.append(write(c, 2))
    for copy in writes:
        copy.wait()


LAST = "y"
FLOPS = 3 * 2 * 1024 * 512 * 512
ANY = pl.BlockSpec(memory_space=pl.ANY)
HBM = pl.BlockSpec(memory_space=pltpu.HBM)
VMEM = pl.BlockSpec(memory_space=pltpu.VMEM)
EVERY = slice(None)


def call(kernel, outs, args, specs, scratch, flops, mib, vmem, out_spec=VMEM):
    return pl.pallas_call(
        kernel,
        out_shape=tuple(jax.ShapeDtypeStruct(s, F32) for s in outs),
        in_specs=specs,
        out_specs=(out_spec,) * len(outs),
        scratch_shapes=scratch,
        compiler_params=pltpu.CompilerParams(vmem_limit_bytes=vmem * 2**20),
        cost_estimate=pl.CostEstimate(flops=flops, bytes_accessed=mib * 2**20, transcendentals=0),
    )(*args)


def joined(outs, args, copies, after=()):
    n, m = len(args), len(after)

    def kernel(*refs):
        for source, part, target, place in copies:
            refs[n + m + target][place] = refs[source][part]

    return call(kernel, outs, (*args, *after), [VMEM] * n + [ANY] * m, [], 0, 1, 4)


def stacked(pieces, after=()):
    size, width = pieces[0].shape
    copies = [
        (k, (EVERY, EVERY), 0, (slice(k * size, (k + 1) * size), EVERY)) for k in range(len(pieces))
    ]
    return joined([(len(pieces) * size, width)], pieces, copies, after)[0]


def first_right(schur, pieces, after):
    shape = schur.shape
    half = (shape[0], HALF)
    scratch = [pltpu.VMEM(shape, F32)] + [pltpu.VMEM((WIN, WIN), BF16)] * 2
    scratch.append(pltpu.SemaphoreType.DMA((4,)))
    specs = [HBM] + [VMEM] * 2 + [ANY] * len(after)
    return call(right_aligned, [half, half], (schur, *pieces, *after), specs, scratch, FLOPS, 5, 12)


def middle_products(parts, r2, l1, after):
    args = (*parts, *r2, *l1)
    scratch = [pltpu.VMEM((2 * WIN, WIN), F32)]
    scratch += [pltpu.VMEM((WIN, WIN), BF16)] * 2 + [pltpu.VMEM((WIN, 2 * WIN), BF16)] * 2
    outs = [(HALF, WIN), (WIN, WIN), (HALF, WIN)]
    specs = [VMEM] * len(args) + [ANY] * len(after)
    return call(middle, outs, (*args, *after), specs, scratch, 2 * FLOPS, 9, 20)


def last_left(parts, l2):
    scratch = [pltpu.VMEM((2 * WIN, WIN), F32)] + [pltpu.VMEM((WIN, 2 * WIN), BF16)] * 2
    scratch.append(pltpu.SemaphoreType.DMA((3,)))
    args = (*parts, *l2)
    outs = [(2 * WIN, WIN)]
    return call(left_shifted, outs, args, [VMEM] * len(args), scratch, FLOPS, 7, 20, HBM)[0]


def gathered(x):
    size = 8
    groups = [[z * size + i for i in range(size)] for z in range(lax.axis_size("col") // size)]
    copies = jnp.broadcast_to(x[None], (size,) + x.shape)
    out = lax.all_to_all(copies, "col", 0, 0, axis_index_groups=groups)
    return out.reshape(size * x.shape[0], x.shape[1])


def ring(x, to):
    perm = [(i, to(i)) for i in range(lax.axis_size("col"))]
    return lax.ppermute(x, "col", perm)


def along_z(by):
    return lambda i: (i + 8 * by) % 32


def around(x, along):
    up = ring(x, along(1))
    down = ring(x, along(-1))
    return x, up, down, ring(up[:64], along(1)), ring(down[64:], along(-1))


def body(schur, left_rot, right_rot, left_off, right_off):
    right = jnp.concatenate([right_rot[0], right_off[0, :, HALF:]], axis=1)
    right = stacked([right, swap(right, "row", 2)])
    right_next = shift(right_off[0, :, :HALF], "col", -1)
    left = gathered(jnp.concatenate([left_rot[0], left_rot[1], left_off[0], left_off[1]], axis=1))
    l1, l2_away, l2 = joined(
        [(128, 2 * WIN), (128, HALF), (128, 2 * WIN - HALF)],
        [left],
        [
            (0, (EVERY, slice(0, 2 * WIN)), 0, (EVERY, EVERY)),
            (0, (EVERY, slice(2 * WIN, 2 * WIN + HALF)), 1, (EVERY, EVERY)),
            (0, (EVERY, slice(2 * WIN + HALF, 4 * WIN)), 2, (EVERY, EVERY)),
        ],
        after=(right_next, right),
    )
    right_core = swap(right, "row", 1)
    right_next = stacked([right_next, swap(right_next, "row", 2)])
    ml, mr = first_right(schur, (right, right_core), (l1,))
    hl = shift(mr, "col", 1)
    hr = shift(ml, "col", -1)
    l1 = around(l1, along_z)
    (l2,) = joined(
        [(128, 2 * WIN)],
        [l2, shift(l2_away, "row", -1)],
        [
            (0, (EVERY, EVERY), 0, (EVERY, slice(0, 2 * WIN - HALF))),
            (1, (EVERY, EVERY), 0, (EVERY, slice(2 * WIN - HALF, 2 * WIN))),
        ],
    )
    next_core = swap(right_next, "row", 1)
    top, mid, low = middle_products(
        (ml, mr, hl, hr), (right, right_core, right_next, next_core), l1, ()
    )
    l2 = around(l2, along_z)
    above = shift(low, "row", 1)
    below = shift(top, "row", -1)
    return last_left((top, mid, low, above, below), l2)


def solution(mesh):
    return jax.shard_map(
        body,
        mesh=mesh,
        in_specs=(
            P("row", "col"),
            P("row", "col", None),
            P("col", "row", None),
            P("row", "col", None),
            P("col", "row", None),
        ),
        out_specs=P("row", "col"),
        check_vma=False,
    )
```

time: 118 us -> 109 us (0.924)
  waiting for transfers between devices: 57.9 us -> 52.5 us
  starting transfers between devices: 43 us -> 39.6 us
    ppermute x20 -> x4, waiting for transfers between devices: 56.1 us -> 22.1 us  [swap(): return lax.ppermute(x, axis, xor_perm(axis, mask))]
    ppermute x0 -> x8, waiting for transfers between devices: none -> 24.1 us  [ring(): return lax.ppermute(x, 'col', perm)]
    ppermute x20 -> x4, starting transfers between devices: 24.6 us -> 2.45 us  [swap(): return lax.ppermute(x, axis, xor_perm(axis, mask))]
    ppermute x0 -> x8, starting transfers between devices: none -> 10.8 us  [ring(): return lax.ppermute(x, 'col', perm)]
    all_to_all x0 -> x1, starting transfers between devices: none -> 6.64 us  [gathered(): out = lax.all_to_all(copies, 'col', 0, 0, axis_index_groups=groups)]
    ppermute x6, waiting for transfers between devices: 1.83 us -> 6.15 us  [shift(): return lax.ppermute(x, axis, shift_perm(axis, by))]
    ppermute x6, starting transfers between devices: 18.5 us -> 19.7 us  [shift(): return lax.ppermute(x, axis, shift_perm(axis, by))]
    unnamed x10 -> x2, local copies, waits for them, and re-layouts: 2.59 us -> 1.59 us
  transfers between devices with their start and end apart: 26 -> 19, of which waited for: 11 -> 9; matrix products, arithmetic and copies ran while one was open for 2% -> 2% of each run, Pallas kernels for 5% -> 4%
where the time goes in v2:
time: 109 us; the launch traced here: 108 us
  waiting for transfers between devices  52.5 us (48%)
  starting transfers between devices  39.6 us (36%)
  Pallas kernels  10.2 us (9%)
  local copies, waits for them, and re-layouts  4.53 us (4%)
    ppermute x8, waiting for transfers between devices, ring(): return lax.ppermute(x, 'col', perm)  24.1 us
    ppermute x4, waiting for transfers between devices, swap(): return lax.ppermute(x, axis, xor_perm(axis, mask))  22.1 us
    ppermute x6, starting transfers between devices, shift(): return lax.ppermute(x, axis, shift_perm(axis, by))  19.7 us
    ppermute x8, starting transfers between devices, ring(): return lax.ppermute(x, 'col', perm)  10.8 us
    pallas_call x7, Pallas kernels, call(): pl.pallas_call(kernel, out_shape=tuple((jax.ShapeDtypeStruct(s, F32) for...  10.2 us
    all_to_all x1, starting transfers between devices, gathered(): out = lax.all_to_all(copies, 'col', 0, 0, axis_index_groups=groups)  6.64 us
    ppermute x6, waiting for transfers between devices, shift(): return lax.ppermute(x, axis, shift_perm(axis, by))  6.15 us
    ppermute x4, starting transfers between devices, swap(): return lax.ppermute(x, axis, xor_perm(axis, mask))  2.45 us
  transfers between devices with their start and end apart: 19, of which 9 were waited for; matrix products, arithmetic and copies ran while one was open for 2% of the time, Pallas kernels for 4%

profile of v2, /device:TPU:0, one launch (start us, length us, event | category | flops | bytes accessed | tf_op | source)
XLA Modules:
  0.0 107.9 jit_solution(259534544997313901)
XLA Ops:
  0.0 1.0 slice_bitcast_fusion
  1.0 1.0 pad_maximum_fusion.refs_0_
  2.0 1.7 %collective-permute-start = (f32[128,768]{1,0:T(8,128)S(1)}, f32[128,768]{1,0:T(8,128)S(1)}, u32[]{:S(2)}, u32[]{:S(2)}) collective-permute-start(f32[128,768]{1,0:T(8,128)S(1)} %pad_maximum_fusion.refs_0_), channel_id=1, source_target_pairs={{0,64},{32,96},{64,0},{96,32},{1,65},{33,97},{65,1},{97,33},{2,66}... | collective-permute-start | bytes 1179656 | tf_op jit(solution)/shard_map/ppermute | solution.py:26
  3.6 0.8 slice_bitcast_fusion.3
  4.5 1.1 broadcast_in_dim.2
  5.5 6.6 %all-to-all-start = ((f32[8,16,2048]{2,1,0:T(8,128)}), f32[8,16,2048]{2,1,0:T(8,128)S(1)}, u32[]{:S(2)}, u32[]{:S(2)}) async-start(f32[8,16,2048]{2,1,0:T(8,128)} %broadcast_in_dim.2), calls=%async_computation | async-start | bytes 2097152 | tf_op jit(solution)/shard_map/all_to_all | solution.py:198
  12.2 0.6 collective-permute-done.refs_1_
  12.8 0.1 collective-permute-start.1
  12.9 9.3 %collective-permute-start.2 = (f32[128,256]{1,0:T(8,128)S(1)}, f32[128,256]{1,0:T(8,128)S(1)}, u32[]{:S(2)}, u32[]{:S(2)}) collective-permute-start(f32[128,256]{1,0:T(8,128)S(1)} %get-tuple-element.21), channel_id=1, source_target_pairs={{0,31},{1,0},{2,1},{3,2},{4,3},{5,4},{6,5},{7,6},{8,7},{9,8},{10,9... | collective-permute-start | bytes 393224 | tf_op jit(solution)/shard_map/ppermute | solution.py:30
  22.2 6.1 %collective-permute-done.2.refs_1_.refs_0_ = f32[128,256]{1,0:T(8,128)S(1)} collective-permute-done((f32[128,256]{1,0:T(8,128)S(1)}, f32[128,256]{1,0:T(8,128)S(1)}, u32[]{:S(2)}, u32[]{:S(2)}) %collective-permute-start.2) | collective-permute-done | bytes 131104 | tf_op jit(solution)/shard_map/ppermute | solution.py:30
  28.3 0.1 all-to-all-done
  28.5 1.6 %copy-done = f32[1024,512]{1,0:T(8,128)S(1)} copy-done((f32[1024,512]{1,0:T(8,128)S(1)}, f32[1024,512]{1,0:T(8,128)}, u32[]{:S(2)}) %copy-start) | copy-done | bytes 2097176
  30.1 2.7 %shard_map.57 = (f32[1024,256]{1,0:T(8,128)S(1)}, f32[1024,256]{1,0:T(8,128)S(1)}) custom-call(f32[1024,512]{1,0:T(8,128)S(1)} %copy-done, f32[256,768]{1,0:T(8,128)S(1)} %shard_map.55.refs_2_.own, f32[256,768]{1,0:T(8,128)S(1)} %collective-permute-done.1.core, f32[128,1024]{1,0:T(8,128)S(1)} %get-tuple-element.13.rest_0_.p0), custom_call_target="tpu_custom_call" | custom-call | flops 1610612736 | bytes 5242880 | tf_op jit(solution)/shard_map/pallas_call | solution.py:139
  32.7 1.7 %collective-permute-start.3 = (f32[1024,256]{1,0:T(8,128)S(1)}, f32[1024,256]{1,0:T(8,128)S(1)}, u32[]{:S(2)}, u32[]{:S(2)}) collective-permute-start(f32[1024,256]{1,0:T(8,128)S(1)} %get-tuple-element.15.mr), channel_id=1, source_target_pairs={{0,1},{1,2},{2,3},{3,4},{4,5},{5,6},{6,7},{7,8},{8,9},{9,10},{10,1... | collective-permute-start | bytes 3145736 | tf_op jit(solution)/shard_map/ppermute | solution.py:30
  34.5 6.1 %collective-permute-start.4 = (f32[1024,256]{1,0:T(8,128)S(1)}, f32[1024,256]{1,0:T(8,128)S(1)}, u32[]{:S(2)}, u32[]{:S(2)}) collective-permute-start(f32[1024,256]{1,0:T(8,128)S(1)} %get-tuple-element.14.ml), channel_id=1, source_target_pairs={{0,31},{1,0},{2,1},{3,2},{4,3},{5,4},{6,5},{7,6},{8,7},{9,8},{10,9... | collective-permute-start | bytes 3145736 | tf_op jit(solution)/shard_map/ppermute | solution.py:30
  40.6 2.8 %collective-permute-start.8 = (f32[128,1024]{1,0:T(8,128)S(1)}, f32[128,1024]{1,0:T(8,128)S(1)}, u32[]{:S(2)}, u32[]{:S(2)}) collective-permute-start(f32[128,1024]{1,0:T(8,128)S(1)} %get-tuple-element.13.rest_0_.p0), channel_id=1, source_target_pairs={{0,24},{1,25},{2,26},{3,27},{4,28},{5,29},{6,30},{7,31},{8,0},{9,1... | collective-permute-start | bytes 1572872 | tf_op jit(solution)/shard_map/ppermute | solution.py:204
  43.4 0.6 collective-permute-start.5
  44.0 21.5 %collective-permute-done.5.refs_1_ = f32[128,256]{1,0:T(8,128)S(1)} collective-permute-done((f32[128,256]{1,0:T(8,128)S(1)}, f32[128,256]{1,0:T(8,128)S(1)}, u32[]{:S(2)}, u32[]{:S(2)}) %collective-permute-start.5) | collective-permute-done | bytes 131104 | tf_op jit(solution)/shard_map/ppermute | solution.py:26
  65.6 0.8 collective-permute-start.13
  66.5 8.2 %collective-permute-done.7.p1 = f32[128,1024]{1,0:T(8,128)S(1)} collective-permute-done((f32[128,1024]{1,0:T(8,128)S(1)}, f32[128,1024]{1,0:T(8,128)S(1)}, u32[]{:S(2)}, u32[]{:S(2)}) %collective-permute-start.7) | collective-permute-done | bytes 524320 | tf_op jit(solution)/shard_map/ppermute | solution.py:204
  74.6 1.3 %collective-permute-start.10 = (f32[64,1024]{1,0:T(8,128)S(1)}, f32[64,1024]{1,0:T(8,128)S(1)}, u32[]{:S(2)}, u32[]{:S(2)}) collective-permute-start(f32[64,1024]{1,0:T(8,128)S(1)} %slice.41), channel_id=1, source_target_pairs={{0,24},{1,25},{2,26},{3,27},{4,28},{5,29},{6,30},{7,31},{8,0},{9,1... | collective-permute-start | bytes 786440 | tf_op jit(solution)/shard_map/ppermute | solution.py:204
  75.9 0.8 collective-permute-start.9
  76.8 0.1 collective-permute-start.14
  76.9 6.0 %collective-permute-done.10.p4 = f32[64,1024]{1,0:T(8,128)S(1)} collective-permute-done((f32[64,1024]{1,0:T(8,128)S(1)}, f32[64,1024]{1,0:T(8,128)S(1)}, u32[]{:S(2)}, u32[]{:S(2)}) %collective-permute-start.10) | collective-permute-done | bytes 262176 | tf_op jit(solution)/shard_map/ppermute | solution.py:204
  82.9 2.5 %collective-permute-start.15 = (f32[128,1024]{1,0:T(8,128)S(1)}, f32[128,1024]{1,0:T(8,128)S(1)}, u32[]{:S(2)}, u32[]{:S(2)}) collective-permute-start(f32[128,1024]{1,0:T(8,128)S(1)} %shard_map.60.p0), channel_id=1, source_target_pairs={{0,24},{1,25},{2,26},{3,27},{4,28},{5,29},{6,30},{7,31},{8,0},{9,1... | collective-permute-start | bytes 1572872 | tf_op jit(solution)/shard_map/ppermute | solution.py:204
  85.4 1.1 %collective-permute-done.9.p3 = f32[64,1024]{1,0:T(8,128)S(1)} collective-permute-done((f32[64,1024]{1,0:T(8,128)S(1)}, f32[64,1024]{1,0:T(8,128)S(1)}, u32[]{:S(2)}, u32[]{:S(2)}) %collective-permute-start.9) | collective-permute-done | bytes 262176 | tf_op jit(solution)/shard_map/ppermute | solution.py:204
  86.4 4.2 %shard_map.59 = (f32[256,512]{1,0:T(8,128)S(1)}, f32[512,512]{1,0:T(8,128)S(1)}, f32[256,512]{1,0:T(8,128)S(1)}) custom-call(f32[1024,256]{1,0:T(8,128)S(1)} %get-tuple-element.14.ml, f32[1024,256]{1,0:T(8,128)S(1)} %get-tuple-element.15.mr, f32[1024,256]{1,0:T(8,128)S(1)} %collective-permute-done.3.hl, f32[1024,256]{1,0:T(8,128)S(1)} %collective-permute-done.4.hr, ...), custom_call_target="tpu_custom_call" | custom-call | flops 3221225472 | bytes 9437184 | tf_op jit(solution)/shard_map/pallas_call | solution.py:139
  90.7 1.7 %collective-permute-start.12 = (f32[256,512]{1,0:T(8,128)S(1)}, f32[256,512]{1,0:T(8,128)S(1)}, u32[]{:S(2)}, u32[]{:S(2)}) collective-permute-start(f32[256,512]{1,0:T(8,128)S(1)} %get-tuple-element.16.top), channel_id=1, source_target_pairs={{0,96},{32,0},{64,32},{96,64},{1,97},{33,1},{65,33},{97,65},{2,98}... | collective-permute-start | bytes 1572872 | tf_op jit(solution)/shard_map/ppermute | solution.py:30
  92.5 4.0 %collective-permute-done.14.p1 = f32[128,1024]{1,0:T(8,128)S(1)} collective-permute-done((f32[128,1024]{1,0:T(8,128)S(1)}, f32[128,1024]{1,0:T(8,128)S(1)}, u32[]{:S(2)}, u32[]{:S(2)}) %collective-permute-start.14) | collective-permute-done | bytes 524320 | tf_op jit(solution)/shard_map/ppermute | solution.py:204
  96.6 3.3 %collective-permute-start.17 = (f32[64,1024]{1,0:T(8,128)S(1)}, f32[64,1024]{1,0:T(8,128)S(1)}, u32[]{:S(2)}, u32[]{:S(2)}) collective-permute-start(f32[64,1024]{1,0:T(8,128)S(1)} %slice.43), channel_id=1, source_target_pairs={{0,24},{1,25},{2,26},{3,27},{4,28},{5,29},{6,30},{7,31},{8,0},{9,1... | collective-permute-start | bytes 786440 | tf_op jit(solution)/shard_map/ppermute | solution.py:204
  99.8 4.9 %collective-permute-done.16.p3 = f32[64,1024]{1,0:T(8,128)S(1)} collective-permute-done((f32[64,1024]{1,0:T(8,128)S(1)}, f32[64,1024]{1,0:T(8,128)S(1)}, u32[]{:S(2)}, u32[]{:S(2)}) %collective-permute-start.16) | collective-permute-done | bytes 262176 | tf_op jit(solution)/shard_map/ppermute | solution.py:204
  104.8 3.1 %shard_map.61 = f32[1024,512]{1,0:T(8,128)} custom-call(f32[256,512]{1,0:T(8,128)S(1)} %get-tuple-element.16.top, f32[512,512]{1,0:T(8,128)S(1)} %get-tuple-element.17.mid, f32[256,512]{1,0:T(8,128)S(1)} %get-tuple-element.18.low, f32[256,512]{1,0:T(8,128)S(1)} %collective-permute-done.11.above, f32[256,512]{1,0:T(8,128)S(1)} %collective-permute-done.12.below, ...), custom_call_target="tpu_custom_call" | custom-call | flops 1610612736 | bytes 7340032 | tf_op jit(solution)/shard_map/pallas_call | solution.py:139
  (24 shorter events, 0.5 us)
Async XLA Ops:
  2.0 10.8 %collective-permute-start = (f32[128,768]{1,0:T(8,128)S(1)}, f32[128,768]{1,0:T(8,128)S(1)}, u32[]{:S(2)}, u32[]{:S(2)}) collective-permute-start(f32[128,768]{1,0:T(8,128)S(1)} %pad_maximum_fusion.refs_0_), channel_id=1, source_target_pairs={{0,64},{32,96},{64,0},{96,32},{1,65},{33,97},{65,1},{97,33},{2,66}... | collective-permute-start | bytes 1179656 | tf_op jit(solution)/shard_map/ppermute | solution.py:26
  5.5 22.9 %all-to-all-start = ((f32[8,16,2048]{2,1,0:T(8,128)}), f32[8,16,2048]{2,1,0:T(8,128)S(1)}, u32[]{:S(2)}, u32[]{:S(2)}) async-start(f32[8,16,2048]{2,1,0:T(8,128)} %broadcast_in_dim.2), calls=%async_computation | async-start | bytes 2097152 | tf_op jit(solution)/shard_map/all_to_all | solution.py:198
  12.8 15.7 %collective-permute-start.1 = (f32[256,768]{1,0:T(8,128)S(1)}, f32[256,768]{1,0:T(8,128)S(1)}, u32[]{:S(2)}, u32[]{:S(2)}) collective-permute-start(f32[256,768]{1,0:T(8,128)S(1)} %shard_map.55.refs_2_.own), channel_id=1, source_target_pairs={{0,32},{32,0},{64,96},{96,64},{1,33},{33,1},{65,97},{97,65},{2,34}... | collective-permute-start | bytes 2359304 | tf_op jit(solution)/shard_map/ppermute | solution.py:26
  12.9 15.4 %collective-permute-start.2 = (f32[128,256]{1,0:T(8,128)S(1)}, f32[128,256]{1,0:T(8,128)S(1)}, u32[]{:S(2)}, u32[]{:S(2)}) collective-permute-start(f32[128,256]{1,0:T(8,128)S(1)} %get-tuple-element.21), channel_id=1, source_target_pairs={{0,31},{1,0},{2,1},{3,2},{4,3},{5,4},{6,5},{7,6},{8,7},{9,8},{10,9... | collective-permute-start | bytes 393224 | tf_op jit(solution)/shard_map/ppermute | solution.py:30
  28.5 1.6 %copy-start = (f32[1024,512]{1,0:T(8,128)S(1)}, f32[1024,512]{1,0:T(8,128)}, u32[]{:S(2)}) copy-start(f32[1024,512]{1,0:T(8,128)} %s.1) | copy-start | bytes 6291460
  32.7 53.7 %collective-permute-start.3 = (f32[1024,256]{1,0:T(8,128)S(1)}, f32[1024,256]{1,0:T(8,128)S(1)}, u32[]{:S(2)}, u32[]{:S(2)}) collective-permute-start(f32[1024,256]{1,0:T(8,128)S(1)} %get-tuple-element.15.mr), channel_id=1, source_target_pairs={{0,1},{1,2},{2,3},{3,4},{4,5},{5,6},{6,7},{7,8},{8,9},{9,10},{10,1... | collective-permute-start | bytes 3145736 | tf_op jit(solution)/shard_map/ppermute | solution.py:30
  34.5 52.0 %collective-permute-start.4 = (f32[1024,256]{1,0:T(8,128)S(1)}, f32[1024,256]{1,0:T(8,128)S(1)}, u32[]{:S(2)}, u32[]{:S(2)}) collective-permute-start(f32[1024,256]{1,0:T(8,128)S(1)} %get-tuple-element.14.ml), channel_id=1, source_target_pairs={{0,31},{1,0},{2,1},{3,2},{4,3},{5,4},{6,5},{7,6},{8,7},{9,8},{10,9... | collective-permute-start | bytes 3145736 | tf_op jit(solution)/shard_map/ppermute | solution.py:30
  40.6 25.8 %collective-permute-start.8 = (f32[128,1024]{1,0:T(8,128)S(1)}, f32[128,1024]{1,0:T(8,128)S(1)}, u32[]{:S(2)}, u32[]{:S(2)}) collective-permute-start(f32[128,1024]{1,0:T(8,128)S(1)} %get-tuple-element.13.rest_0_.p0), channel_id=1, source_target_pairs={{0,24},{1,25},{2,26},{3,27},{4,28},{5,29},{6,30},{7,31},{8,0},{9,1... | collective-permute-start | bytes 1572872 | tf_op jit(solution)/shard_map/ppermute | solution.py:204
  43.4 31.2 %collective-permute-start.7 = (f32[128,1024]{1,0:T(8,128)S(1)}, f32[128,1024]{1,0:T(8,128)S(1)}, u32[]{:S(2)}, u32[]{:S(2)}) collective-permute-start(f32[128,1024]{1,0:T(8,128)S(1)} %get-tuple-element.13.rest_0_.p0), channel_id=1, source_target_pairs={{0,8},{1,9},{2,10},{3,11},{4,12},{5,13},{6,14},{7,15},{8,16},{9,17... | collective-permute-start | bytes 1572872 | tf_op jit(solution)/shard_map/ppermute | solution.py:204
  43.4 22.2 %collective-permute-start.5 = (f32[128,256]{1,0:T(8,128)S(1)}, f32[128,256]{1,0:T(8,128)S(1)}, u32[]{:S(2)}, u32[]{:S(2)}) collective-permute-start(f32[128,256]{1,0:T(8,128)S(1)} %collective-permute-done.2.refs_1_.refs_0_), channel_id=1, source_target_pairs={{0,64},{32,96},{64,0},{96,32},{1,65},{33,97},{65,1},{97,33},{2,66}... | collective-permute-start | bytes 393224 | tf_op jit(solution)/shard_map/ppermute | solution.py:26
  65.6 10.4 %collective-permute-start.13 = (f32[128,256]{1,0:T(8,128)S(1)}, f32[128,256]{1,0:T(8,128)S(1)}, u32[]{:S(2)}, u32[]{:S(2)}) collective-permute-start(f32[128,256]{1,0:T(8,128)S(1)} %get-tuple-element.20), channel_id=1, source_target_pairs={{0,96},{32,0},{64,32},{96,64},{1,97},{33,1},{65,33},{97,65},{2,98}... | collective-permute-start | bytes 393224 | tf_op jit(solution)/shard_map/ppermute | solution.py:30
  66.4 10.4 %collective-permute-start.6 = (f32[256,256]{1,0:T(8,128)S(1)}, f32[256,256]{1,0:T(8,128)S(1)}, u32[]{:S(2)}, u32[]{:S(2)}) collective-permute-start(f32[256,256]{1,0:T(8,128)S(1)} %shard_map.58.next_own), channel_id=1, source_target_pairs={{0,32},{32,0},{64,96},{96,64},{1,33},{33,1},{65,97},{97,65},{2,34}... | collective-permute-start | bytes 786440 | tf_op jit(solution)/shard_map/ppermute | solution.py:26
  74.6 8.2 %collective-permute-start.10 = (f32[64,1024]{1,0:T(8,128)S(1)}, f32[64,1024]{1,0:T(8,128)S(1)}, u32[]{:S(2)}, u32[]{:S(2)}) collective-permute-start(f32[64,1024]{1,0:T(8,128)S(1)} %slice.41), channel_id=1, source_target_pairs={{0,24},{1,25},{2,26},{3,27},{4,28},{5,29},{6,30},{7,31},{8,0},{9,1... | collective-permute-start | bytes 786440 | tf_op jit(solution)/shard_map/ppermute | solution.py:204
  75.9 10.5 %collective-permute-start.9 = (f32[64,1024]{1,0:T(8,128)S(1)}, f32[64,1024]{1,0:T(8,128)S(1)}, u32[]{:S(2)}, u32[]{:S(2)}) collective-permute-start(f32[64,1024]{1,0:T(8,128)S(1)} %slice.40), channel_id=1, source_target_pairs={{0,8},{1,9},{2,10},{3,11},{4,12},{5,13},{6,14},{7,15},{8,16},{9,17... | collective-permute-start | bytes 786440 | tf_op jit(solution)/shard_map/ppermute | solution.py:204
  76.8 19.6 %collective-permute-start.14 = (f32[128,1024]{1,0:T(8,128)S(1)}, f32[128,1024]{1,0:T(8,128)S(1)}, u32[]{:S(2)}, u32[]{:S(2)}) collective-permute-start(f32[128,1024]{1,0:T(8,128)S(1)} %shard_map.60.p0), channel_id=1, source_target_pairs={{0,8},{1,9},{2,10},{3,11},{4,12},{5,13},{6,14},{7,15},{8,16},{9,17... | collective-permute-start | bytes 1572872 | tf_op jit(solution)/shard_map/ppermute | solution.py:204
  82.9 13.6 %collective-permute-start.15 = (f32[128,1024]{1,0:T(8,128)S(1)}, f32[128,1024]{1,0:T(8,128)S(1)}, u32[]{:S(2)}, u32[]{:S(2)}) collective-permute-start(f32[128,1024]{1,0:T(8,128)S(1)} %shard_map.60.p0), channel_id=1, source_target_pairs={{0,24},{1,25},{2,26},{3,27},{4,28},{5,29},{6,30},{7,31},{8,0},{9,1... | collective-permute-start | bytes 1572872 | tf_op jit(solution)/shard_map/ppermute | solution.py:204
  90.6 14.1 %collective-permute-start.11 = (f32[256,512]{1,0:T(8,128)S(1)}, f32[256,512]{1,0:T(8,128)S(1)}, u32[]{:S(2)}, u32[]{:S(2)}) collective-permute-start(f32[256,512]{1,0:T(8,128)S(1)} %get-tuple-element.18.low), channel_id=1, source_target_pairs={{0,32},{32,64},{64,96},{96,0},{1,33},{33,65},{65,97},{97,1},{2,34}... | collective-permute-start | bytes 1572872 | tf_op jit(solution)/shard_map/ppermute | solution.py:30
  90.7 14.1 %collective-permute-start.12 = (f32[256,512]{1,0:T(8,128)S(1)}, f32[256,512]{1,0:T(8,128)S(1)}, u32[]{:S(2)}, u32[]{:S(2)}) collective-permute-start(f32[256,512]{1,0:T(8,128)S(1)} %get-tuple-element.16.top), channel_id=1, source_target_pairs={{0,96},{32,0},{64,32},{96,64},{1,97},{33,1},{65,33},{97,65},{2,98}... | collective-permute-start | bytes 1572872 | tf_op jit(solution)/shard_map/ppermute | solution.py:30
  96.4 8.3 %collective-permute-start.16 = (f32[64,1024]{1,0:T(8,128)S(1)}, f32[64,1024]{1,0:T(8,128)S(1)}, u32[]{:S(2)}, u32[]{:S(2)}) collective-permute-start(f32[64,1024]{1,0:T(8,128)S(1)} %slice.42), channel_id=1, source_target_pairs={{0,8},{1,9},{2,10},{3,11},{4,12},{5,13},{6,14},{7,15},{8,16},{9,17... | collective-permute-start | bytes 786440 | tf_op jit(solution)/shard_map/ppermute | solution.py:204
  96.6 8.2 %collective-permute-start.17 = (f32[64,1024]{1,0:T(8,128)S(1)}, f32[64,1024]{1,0:T(8,128)S(1)}, u32[]{:S(2)}, u32[]{:S(2)}) collective-permute-start(f32[64,1024]{1,0:T(8,128)S(1)} %slice.43), channel_id=1, source_target_pairs={{0,24},{1,25},{2,26},{3,27},{4,28},{5,29},{6,30},{7,31},{8,0},{9,1... | collective-permute-start | bytes 786440 | tf_op jit(solution)/shard_map/ppermute | solution.py:204

commit v3 on v2

--- a/solution.py
+++ b/solution.py
@@ -191,6 +191,12 @@
     return call(left_shifted, outs, args, [VMEM] * len(args), scratch, FLOPS, 7, 20, HBM)[0]
 
 
+def across_next(x):
+    rows, cols = lax.axis_size("row"), lax.axis_size("col")
+    perm = [(r * cols + c, (r ^ 2) * cols + (c - 1) % cols) for r in range(rows) for c in range(cols)]
+    return lax.ppermute(x, ("row", "col"), perm)
+
+
 def gathered(x):
     size = 8
     groups = [[z * size + i for i in range(size)] for z in range(lax.axis_size("col") // size)]
@@ -215,34 +221,28 @@
 
 
 def body(schur, left_rot, right_rot, left_off, right_off):
-    right = jnp.concatenate([right_rot[0], right_off[0, :, HALF:]], axis=1)
-    right = stacked([right, swap(right, "row", 2)])
-    right_next = shift(right_off[0, :, :HALF], "col", -1)
-    left = gathered(jnp.concatenate([left_rot[0], left_rot[1], left_off[0], left_off[1]], axis=1))
-    l1, l2_away, l2 = joined(
-        [(128, 2 * WIN), (128, HALF), (128, 2 * WIN - HALF)],
-        [left],
-        [
-            (0, (EVERY, slice(0, 2 * WIN)), 0, (EVERY, EVERY)),
-            (0, (EVERY, slice(2 * WIN, 2 * WIN + HALF)), 1, (EVERY, EVERY)),
-            (0, (EVERY, slice(2 * WIN + HALF, 4 * WIN)), 2, (EVERY, EVERY)),
-        ],
-        after=(right_next, right),
-    )
-    right_core = swap(right, "row", 1)
-    right_next = stacked([right_next, swap(right_next, "row", 2)])
-    ml, mr = first_right(schur, (right, right_core), (l1,))
-    hl = shift(mr, "col", 1)
-    hr = shift(ml, "col", -1)
+    l1 = gathered(jnp.concatenate([left_rot[0], left_rot[1]], axis=1))
     l1 = around(l1, along_z)
+    right_next = right_off[0, :, :HALF]
+    right_next = stacked([shift(right_next, "col", -1), across_next(right_next)])
+    away = shift(left_off[0, :, :HALF], "row", -1)
+    l2 = jnp.concatenate([left_off[0, :, HALF:], left_off[1]], axis=1)
     (l2,) = joined(
-        [(128, 2 * WIN)],
-        [l2, shift(l2_away, "row", -1)],
+        [(16, 2 * WIN)],
+        [l2, away],
         [
             (0, (EVERY, EVERY), 0, (EVERY, slice(0, 2 * WIN - HALF))),
             (1, (EVERY, EVERY), 0, (EVERY, slice(2 * WIN - HALF, 2 * WIN))),
         ],
+        after=(right_next,),
     )
+    l2 = gathered(l2)
+    right = jnp.concatenate([right_rot[0], right_off[0, :, HALF:]], axis=1)
+    right = stacked([right, swap(right, "row", 2)])
+    right_core = swap(right, "row", 1)
+    ml, mr = first_right(schur, (right, right_core), (l2, l1[1], l1[2]))
+    hl = shift(mr, "col", 1)
+    hr = shift(ml, "col", -1)
     next_core = swap(right_next, "row", 1)
     top, mid, low = middle_products(
         (ml, mr, hl, hr), (right, right_core, right_next, next_core), l1, ()

time: 109 us -> 108 us (level)
  blocking collectives: 0 us -> 17.2 us
  waiting for transfers between devices: 52.5 us -> 38.1 us
  local copies, waits for them, and re-layouts: 4.53 us -> 2.77 us
  starting transfers between devices: 39.6 us -> 38.5 us
    ppermute x4 -> x3, waiting for transfers between devices: 22.1 us -> 0.01 us  [swap(): return lax.ppermute(x, axis, xor_perm(axis, mask))]
    all_to_all x0 -> x1, blocking collectives: none -> 17.2 us  [gathered(): out = lax.all_to_all(copies, 'col', 0, 0, axis_index_groups=groups)]
    ppermute x8, waiting for transfers between devices: 24.1 us -> 36.4 us  [ring(): return lax.ppermute(x, 'col', perm)]
    ppermute x6, waiting for transfers between devices: 6.15 us -> 0.02 us  [shift(): return lax.ppermute(x, axis, shift_perm(axis, by))]
    unnamed x2 -> x4, local copies, waits for them, and re-layouts: 1.59 us -> 0.01 us
    all_to_all x1, waiting for transfers between devices: 0.1 us -> 1.66 us  [gathered(): out = lax.all_to_all(copies, 'col', 0, 0, axis_index_groups=groups)]
    ppermute x4 -> x3, starting transfers between devices: 2.45 us -> 2.22 us  [swap(): return lax.ppermute(x, axis, xor_perm(axis, mask))]
    pallas_call x7 -> x6, Pallas kernels: 10.2 us -> 10.1 us  [call(): pl.pallas_call(kernel, out_shape=tuple((jax.ShapeDtypeStruct(s, F32) for...]
  transfers between devices with their start and end apart: 19 -> 19, of which waited for: 9 -> 6; matrix products, arithmetic and copies ran while one was open for 2% -> 2% of each run, Pallas kernels for 4% -> 4%
where the time goes in v3:
time: 108 us
  starting transfers between devices  38.5 us (36%)
  waiting for transfers between devices  38.1 us (35%)
  blocking collectives  17.2 us (16%)
  Pallas kernels  10.1 us (9%)
  local copies, waits for them, and re-layouts  2.77 us (3%)
    ppermute x8, waiting for transfers between devices, ring(): return lax.ppermute(x, 'col', perm)  36.4 us
    ppermute x6, starting transfers between devices, shift(): return lax.ppermute(x, axis, shift_perm(axis, by))  18.7 us
    all_to_all x1, blocking collectives, gathered(): out = lax.all_to_all(copies, 'col', 0, 0, axis_index_groups=groups)  17.2 us
    ppermute x8, starting transfers between devices, ring(): return lax.ppermute(x, 'col', perm)  10.7 us
    pallas_call x6, Pallas kernels, call(): pl.pallas_call(kernel, out_shape=tuple((jax.ShapeDtypeStruct(s, F32) for...  10.1 us
    all_to_all x1, starting transfers between devices, gathered(): out = lax.all_to_all(copies, 'col', 0, 0, axis_index_groups=groups)  6.64 us
    ppermute x3, starting transfers between devices, swap(): return lax.ppermute(x, axis, xor_perm(axis, mask))  2.22 us
  transfers between devices with their start and end apart: 19, of which 6 were waited for; matrix products, arithmetic and copies ran while one was open for 2% of the time, Pallas kernels for 4%

profile of v3, /device:TPU:0, one launch (start us, length us, event | category | flops | bytes accessed | tf_op | source)
XLA Modules:
  0.0 107.9 jit_solution(16849030418593464452)
XLA Ops:
  0.0 1.0 slice_bitcast_fusion
  1.0 1.0 pad_maximum_fusion.refs_0_
  2.0 1.7 %collective-permute-start = (f32[128,768]{1,0:T(8,128)S(1)}, f32[128,768]{1,0:T(8,128)S(1)}, u32[]{:S(2)}, u32[]{:S(2)}) collective-permute-start(f32[128,768]{1,0:T(8,128)S(1)} %pad_maximum_fusion.refs_0_), channel_id=1, source_target_pairs={{0,64},{32,96},{64,0},{96,32},{1,65},{33,97},{65,1},{97,33},{2,66}... | collective-permute-start | bytes 1179656 | tf_op jit(solution)/shard_map/ppermute | solution.py:26
  3.7 0.8 slice_bitcast_fusion.3
  4.4 0.8 broadcast_in_dim.5
  5.3 6.6 %all-to-all-start.1 = ((f32[8,16,1024]{2,1,0:T(8,128)}), f32[8,16,1024]{2,1,0:T(8,128)S(1)}, u32[]{:S(2)}, u32[]{:S(2)}) async-start(f32[8,16,1024]{2,1,0:T(8,128)} %broadcast_in_dim.5), calls=%async_computation.1 | async-start | bytes 1048576 | tf_op jit(solution)/shard_map/all_to_all | solution.py:204
  11.9 9.1 %collective-permute-start.3 = (f32[128,256]{1,0:T(8,128)S(1)}, f32[128,256]{1,0:T(8,128)S(1)}, u32[]{:S(2)}, u32[]{:S(2)}) collective-permute-start(f32[128,256]{1,0:T(8,128)S(1)} %get-tuple-element.15), channel_id=1, source_target_pairs={{0,31},{1,0},{2,1},{3,2},{4,3},{5,4},{6,5},{7,6},{8,7},{9,8},{10,9... | collective-permute-start | bytes 393224 | tf_op jit(solution)/shard_map/ppermute | solution.py:30
  21.0 0.2 collective-permute-start.4
  21.3 0.0 collective-permute-done.refs_1_
  21.3 0.1 shard_map.55.own
  21.4 0.6 collective-permute-start.1
  21.9 1.7 %all-to-all-done.1 = f32[8,16,1024]{2,1,0:T(8,128)S(1)} async-done(((f32[8,16,1024]{2,1,0:T(8,128)}), f32[8,16,1024]{2,1,0:T(8,128)S(1)}, u32[]{:S(2)}, u32[]{:S(2)}) %all-to-all-start.1) | async-done | bytes 524320 | tf_op jit(solution)/shard_map/all_to_all | solution.py:204
  23.6 1.9 %collective-permute-start.5 = (f32[128,1024]{1,0:T(8,128)S(1)}, f32[128,1024]{1,0:T(8,128)S(1)}, u32[]{:S(2)}, u32[]{:S(2)}) collective-permute-start(f32[128,1024]{1,0:T(8,128)S(1)} %bitcast.21), channel_id=1, source_target_pairs={{0,8},{1,9},{2,10},{3,11},{4,12},{5,13},{6,14},{7,15},{8,16},{9,17... | collective-permute-start | bytes 1572872 | tf_op jit(solution)/shard_map/ppermute | solution.py:210
  25.5 3.8 %collective-permute-start.6 = (f32[128,1024]{1,0:T(8,128)S(1)}, f32[128,1024]{1,0:T(8,128)S(1)}, u32[]{:S(2)}, u32[]{:S(2)}) collective-permute-start(f32[128,1024]{1,0:T(8,128)S(1)} %bitcast.22), channel_id=1, source_target_pairs={{0,24},{1,25},{2,26},{3,27},{4,28},{5,29},{6,30},{7,31},{8,0},{9,1... | collective-permute-start | bytes 1572872 | tf_op jit(solution)/shard_map/ppermute | solution.py:210
  29.3 0.0 collective-permute-done.4.refs_1_
  29.4 17.2 %all_to_all.10 = f32[8,16,1024]{2,1,0:T(8,128)S(1)} all-to-all(f32[8,16,1024]{2,1,0:T(8,128)S(1)} %broadcast_in_dim.4), channel_id=1, replica_groups={{0,1,2,3,4,5,6,7},{8,9,10,11,12,13,14,15},{16,17,18,19,20,21,22,23},{24..., dimensions={0} | all-to-all | bytes 1048576 | tf_op jit(solution)/shard_map/all_to_all | solution.py:204
  46.6 2.7 %shard_map.58 = (f32[1024,256]{1,0:T(8,128)S(1)}, f32[1024,256]{1,0:T(8,128)S(1)}) custom-call(f32[1024,512]{1,0:T(8,128)S(1)} %copy-done, f32[256,768]{1,0:T(8,128)S(1)} %shard_map.55.own, f32[256,768]{1,0:T(8,128)S(1)} %collective-permute-done.1.core, f32[128,1024]{1,0:T(8,128)S(1)} %bitcast.17, f32[128,1024]{1,0:T(8,128)S(1)} %collective-permute-done.5.rest_1_.p1, ...), custom_call_target="tpu_custom_call" | custom-call | flops 1610612736 | bytes 5242880 | tf_op jit(solution)/shard_map/pallas_call | solution.py:139
  49.3 0.3 collective-permute-start.7
  49.6 7.5 %collective-permute-start.8 = (f32[1024,256]{1,0:T(8,128)S(1)}, f32[1024,256]{1,0:T(8,128)S(1)}, u32[]{:S(2)}, u32[]{:S(2)}) collective-permute-start(f32[1024,256]{1,0:T(8,128)S(1)} %get-tuple-element.10.ml), channel_id=1, source_target_pairs={{0,31},{1,0},{2,1},{3,2},{4,3},{5,4},{6,5},{7,6},{8,7},{9,8},{10,9... | collective-permute-start | bytes 3145736 | tf_op jit(solution)/shard_map/ppermute | solution.py:30
  57.2 0.1 collective-permute-start.10
  57.3 3.3 %collective-permute-start.11 = (f32[64,1024]{1,0:T(8,128)S(1)}, f32[64,1024]{1,0:T(8,128)S(1)}, u32[]{:S(2)}, u32[]{:S(2)}) collective-permute-start(f32[64,1024]{1,0:T(8,128)S(1)} %slice.45), channel_id=1, source_target_pairs={{0,24},{1,25},{2,26},{3,27},{4,28},{5,29},{6,30},{7,31},{8,0},{9,1... | collective-permute-start | bytes 786440 | tf_op jit(solution)/shard_map/ppermute | solution.py:210
  60.6 22.8 %collective-permute-done.10.p3 = f32[64,1024]{1,0:T(8,128)S(1)} collective-permute-done((f32[64,1024]{1,0:T(8,128)S(1)}, f32[64,1024]{1,0:T(8,128)S(1)}, u32[]{:S(2)}, u32[]{:S(2)}) %collective-permute-start.10) | collective-permute-done | bytes 262176 | tf_op jit(solution)/shard_map/ppermute | solution.py:210
  83.4 4.2 %shard_map.59 = (f32[256,512]{1,0:T(8,128)S(1)}, f32[512,512]{1,0:T(8,128)S(1)}, f32[256,512]{1,0:T(8,128)S(1)}) custom-call(f32[1024,256]{1,0:T(8,128)S(1)} %get-tuple-element.10.ml, f32[1024,256]{1,0:T(8,128)S(1)} %get-tuple-element.11.mr, f32[1024,256]{1,0:T(8,128)S(1)} %collective-permute-done.7.hl, f32[1024,256]{1,0:T(8,128)S(1)} %collective-permute-done.8.hr, ...), custom_call_target="tpu_custom_call" | custom-call | flops 3221225472 | bytes 9437184 | tf_op jit(solution)/shard_map/pallas_call | solution.py:139
  87.6 0.1 collective-permute-start.12
  87.7 1.7 %collective-permute-start.13 = (f32[256,512]{1,0:T(8,128)S(1)}, f32[256,512]{1,0:T(8,128)S(1)}, u32[]{:S(2)}, u32[]{:S(2)}) collective-permute-start(f32[256,512]{1,0:T(8,128)S(1)} %get-tuple-element.12.top), channel_id=1, source_target_pairs={{0,96},{32,0},{64,32},{96,64},{1,97},{33,1},{65,33},{97,65},{2,98}... | collective-permute-start | bytes 1572872 | tf_op jit(solution)/shard_map/ppermute | solution.py:30
  89.4 5.1 %collective-permute-done.14.p1 = f32[128,1024]{1,0:T(8,128)S(1)} collective-permute-done((f32[128,1024]{1,0:T(8,128)S(1)}, f32[128,1024]{1,0:T(8,128)S(1)}, u32[]{:S(2)}, u32[]{:S(2)}) %collective-permute-start.14) | collective-permute-done | bytes 524320 | tf_op jit(solution)/shard_map/ppermute | solution.py:210
  94.6 0.1 collective-permute-start.16
  94.7 2.6 %collective-permute-done.15.p2 = f32[128,1024]{1,0:T(8,128)S(1)} collective-permute-done((f32[128,1024]{1,0:T(8,128)S(1)}, f32[128,1024]{1,0:T(8,128)S(1)}, u32[]{:S(2)}, u32[]{:S(2)}) %collective-permute-start.15) | collective-permute-done | bytes 524320 | tf_op jit(solution)/shard_map/ppermute | solution.py:210
  97.3 1.6 %collective-permute-start.17 = (f32[64,1024]{1,0:T(8,128)S(1)}, f32[64,1024]{1,0:T(8,128)S(1)}, u32[]{:S(2)}, u32[]{:S(2)}) collective-permute-start(f32[64,1024]{1,0:T(8,128)S(1)} %slice.47), channel_id=1, source_target_pairs={{0,24},{1,25},{2,26},{3,27},{4,28},{5,29},{6,30},{7,31},{8,0},{9,1... | collective-permute-start | bytes 786440 | tf_op jit(solution)/shard_map/ppermute | solution.py:210
  98.8 5.3 %collective-permute-done.16.p3 = f32[64,1024]{1,0:T(8,128)S(1)} collective-permute-done((f32[64,1024]{1,0:T(8,128)S(1)}, f32[64,1024]{1,0:T(8,128)S(1)}, u32[]{:S(2)}, u32[]{:S(2)}) %collective-permute-start.16) | collective-permute-done | bytes 262176 | tf_op jit(solution)/shard_map/ppermute | solution.py:210
  104.2 0.6 collective-permute-done.17.p4
  104.7 3.1 %shard_map.60 = f32[1024,512]{1,0:T(8,128)} custom-call(f32[256,512]{1,0:T(8,128)S(1)} %get-tuple-element.12.top, f32[512,512]{1,0:T(8,128)S(1)} %get-tuple-element.13.mid, f32[256,512]{1,0:T(8,128)S(1)} %get-tuple-element.14.low, f32[256,512]{1,0:T(8,128)S(1)} %collective-permute-done.12.above, f32[256,512]{1,0:T(8,128)S(1)} %collective-permute-done.13.below, ...), custom_call_target="tpu_custom_call" | custom-call | flops 1610612736 | bytes 7340032 | tf_op jit(solution)/shard_map/pallas_call | solution.py:139
  (30 shorter events, 0.2 us)
Async XLA Ops:
  0.0 21.3 %copy-start.1 = (f32[2,16,512]{2,1,0:T(8,128)S(1)}, f32[2,16,512]{2,1,0:T(8,128)}, u32[]{:S(2)}) copy-start(f32[2,16,512]{2,1,0:T(8,128)} %param.8) | copy-start | bytes 196612
  2.0 19.3 %collective-permute-start = (f32[128,768]{1,0:T(8,128)S(1)}, f32[128,768]{1,0:T(8,128)S(1)}, u32[]{:S(2)}, u32[]{:S(2)}) collective-permute-start(f32[128,768]{1,0:T(8,128)S(1)} %pad_maximum_fusion.refs_0_), channel_id=1, source_target_pairs={{0,64},{32,96},{64,0},{96,32},{1,65},{33,97},{65,1},{97,33},{2,66}... | collective-permute-start | bytes 1179656 | tf_op jit(solution)/shard_map/ppermute | solution.py:26
  5.3 18.3 %all-to-all-start.1 = ((f32[8,16,1024]{2,1,0:T(8,128)}), f32[8,16,1024]{2,1,0:T(8,128)S(1)}, u32[]{:S(2)}, u32[]{:S(2)}) async-start(f32[8,16,1024]{2,1,0:T(8,128)} %broadcast_in_dim.5), calls=%async_computation.1 | async-start | bytes 1048576 | tf_op jit(solution)/shard_map/all_to_all | solution.py:204
  11.9 13.6 %collective-permute-start.3 = (f32[128,256]{1,0:T(8,128)S(1)}, f32[128,256]{1,0:T(8,128)S(1)}, u32[]{:S(2)}, u32[]{:S(2)}) collective-permute-start(f32[128,256]{1,0:T(8,128)S(1)} %get-tuple-element.15), channel_id=1, source_target_pairs={{0,31},{1,0},{2,1},{3,2},{4,3},{5,4},{6,5},{7,6},{8,7},{9,8},{10,9... | collective-permute-start | bytes 393224 | tf_op jit(solution)/shard_map/ppermute | solution.py:30
  21.0 8.2 %collective-permute-start.4 = (f32[128,256]{1,0:T(8,128)S(1)}, f32[128,256]{1,0:T(8,128)S(1)}, u32[]{:S(2)}, u32[]{:S(2)}) collective-permute-start(f32[128,256]{1,0:T(8,128)S(1)} %get-tuple-element.15), channel_id=1, source_target_pairs={{0,95},{1,64},{2,65},{3,66},{4,67},{5,68},{6,69},{7,70},{8,71},{9,... | collective-permute-start | bytes 393224 | tf_op jit(solution)/shard_map/ppermute | solution.py:197
  21.3 8.0 %collective-permute-start.2 = (f32[16,256]{1,0:T(8,128)S(1)}, f32[16,256]{1,0:T(8,128)S(1)}, u32[]{:S(2)}, u32[]{:S(2)}) collective-permute-start(f32[16,256]{1,0:T(8,128)S(1)} %get-tuple-element.19), channel_id=1, source_target_pairs={{0,96},{32,0},{64,32},{96,64},{1,97},{33,1},{65,33},{97,65},{2,98}... | collective-permute-start | bytes 49160 | tf_op jit(solution)/shard_map/ppermute | solution.py:30
  21.4 25.3 %collective-permute-start.1 = (f32[256,768]{1,0:T(8,128)S(1)}, f32[256,768]{1,0:T(8,128)S(1)}, u32[]{:S(2)}, u32[]{:S(2)}) collective-permute-start(f32[256,768]{1,0:T(8,128)S(1)} %shard_map.55.own), channel_id=1, source_target_pairs={{0,32},{32,0},{64,96},{96,64},{1,33},{33,1},{65,97},{97,65},{2,34}... | collective-permute-start | bytes 2359304 | tf_op jit(solution)/shard_map/ppermute | solution.py:26
  23.6 23.0 %copy-start = (f32[1024,512]{1,0:T(8,128)S(1)}, f32[1024,512]{1,0:T(8,128)}, u32[]{:S(2)}) copy-start(f32[1024,512]{1,0:T(8,128)} %s.1) | copy-start | bytes 6291460
  23.6 23.0 %collective-permute-start.5 = (f32[128,1024]{1,0:T(8,128)S(1)}, f32[128,1024]{1,0:T(8,128)S(1)}, u32[]{:S(2)}, u32[]{:S(2)}) collective-permute-start(f32[128,1024]{1,0:T(8,128)S(1)} %bitcast.21), channel_id=1, source_target_pairs={{0,8},{1,9},{2,10},{3,11},{4,12},{5,13},{6,14},{7,15},{8,16},{9,17... | collective-permute-start | bytes 1572872 | tf_op jit(solution)/shard_map/ppermute | solution.py:210
  25.5 21.1 %collective-permute-start.6 = (f32[128,1024]{1,0:T(8,128)S(1)}, f32[128,1024]{1,0:T(8,128)S(1)}, u32[]{:S(2)}, u32[]{:S(2)}) collective-permute-start(f32[128,1024]{1,0:T(8,128)S(1)} %bitcast.22), channel_id=1, source_target_pairs={{0,24},{1,25},{2,26},{3,27},{4,28},{5,29},{6,30},{7,31},{8,0},{9,1... | collective-permute-start | bytes 1572872 | tf_op jit(solution)/shard_map/ppermute | solution.py:210
  49.3 34.1 %collective-permute-start.7 = (f32[1024,256]{1,0:T(8,128)S(1)}, f32[1024,256]{1,0:T(8,128)S(1)}, u32[]{:S(2)}, u32[]{:S(2)}) collective-permute-start(f32[1024,256]{1,0:T(8,128)S(1)} %get-tuple-element.11.mr), channel_id=1, source_target_pairs={{0,1},{1,2},{2,3},{3,4},{4,5},{5,6},{6,7},{7,8},{8,9},{9,10},{10,1... | collective-permute-start | bytes 3145736 | tf_op jit(solution)/shard_map/ppermute | solution.py:30
  49.6 33.8 %collective-permute-start.8 = (f32[1024,256]{1,0:T(8,128)S(1)}, f32[1024,256]{1,0:T(8,128)S(1)}, u32[]{:S(2)}, u32[]{:S(2)}) collective-permute-start(f32[1024,256]{1,0:T(8,128)S(1)} %get-tuple-element.10.ml), channel_id=1, source_target_pairs={{0,31},{1,0},{2,1},{3,2},{4,3},{5,4},{6,5},{7,6},{8,7},{9,8},{10,9... | collective-permute-start | bytes 3145736 | tf_op jit(solution)/shard_map/ppermute | solution.py:30
  57.1 3.4 %collective-permute-start.9 = (f32[256,256]{1,0:T(8,128)S(1)}, f32[256,256]{1,0:T(8,128)S(1)}, u32[]{:S(2)}, u32[]{:S(2)}) collective-permute-start(f32[256,256]{1,0:T(8,128)S(1)} %shard_map.56.refs_2_.next_own), channel_id=1, source_target_pairs={{0,32},{32,0},{64,96},{96,64},{1,33},{33,1},{65,97},{97,65},{2,34}... | collective-permute-start | bytes 786440 | tf_op jit(solution)/shard_map/ppermute | solution.py:26
  57.2 26.2 %collective-permute-start.10 = (f32[64,1024]{1,0:T(8,128)S(1)}, f32[64,1024]{1,0:T(8,128)S(1)}, u32[]{:S(2)}, u32[]{:S(2)}) collective-permute-start(f32[64,1024]{1,0:T(8,128)S(1)} %slice.44), channel_id=1, source_target_pairs={{0,8},{1,9},{2,10},{3,11},{4,12},{5,13},{6,14},{7,15},{8,16},{9,17... | collective-permute-start | bytes 786440 | tf_op jit(solution)/shard_map/ppermute | solution.py:210
  57.3 26.1 %collective-permute-start.11 = (f32[64,1024]{1,0:T(8,128)S(1)}, f32[64,1024]{1,0:T(8,128)S(1)}, u32[]{:S(2)}, u32[]{:S(2)}) collective-permute-start(f32[64,1024]{1,0:T(8,128)S(1)} %slice.45), channel_id=1, source_target_pairs={{0,24},{1,25},{2,26},{3,27},{4,28},{5,29},{6,30},{7,31},{8,0},{9,1... | collective-permute-start | bytes 786440 | tf_op jit(solution)/shard_map/ppermute | solution.py:210
  60.6 34.0 %collective-permute-start.14 = (f32[128,1024]{1,0:T(8,128)S(1)}, f32[128,1024]{1,0:T(8,128)S(1)}, u32[]{:S(2)}, u32[]{:S(2)}) collective-permute-start(f32[128,1024]{1,0:T(8,128)S(1)} %bitcast.18), channel_id=1, source_target_pairs={{0,8},{1,9},{2,10},{3,11},{4,12},{5,13},{6,14},{7,15},{8,16},{9,17... | collective-permute-start | bytes 1572872 | tf_op jit(solution)/shard_map/ppermute | solution.py:210
  83.4 13.9 %collective-permute-start.15 = (f32[128,1024]{1,0:T(8,128)S(1)}, f32[128,1024]{1,0:T(8,128)S(1)}, u32[]{:S(2)}, u32[]{:S(2)}) collective-permute-start(f32[128,1024]{1,0:T(8,128)S(1)} %bitcast.19), channel_id=1, source_target_pairs={{0,24},{1,25},{2,26},{3,27},{4,28},{5,29},{6,30},{7,31},{8,0},{9,1... | collective-permute-start | bytes 1572872 | tf_op jit(solution)/shard_map/ppermute | solution.py:210
  87.6 17.1 %collective-permute-start.12 = (f32[256,512]{1,0:T(8,128)S(1)}, f32[256,512]{1,0:T(8,128)S(1)}, u32[]{:S(2)}, u32[]{:S(2)}) collective-permute-start(f32[256,512]{1,0:T(8,128)S(1)} %get-tuple-element.14.low), channel_id=1, source_target_pairs={{0,32},{32,64},{64,96},{96,0},{1,33},{33,65},{65,97},{97,1},{2,34}... | collective-permute-start | bytes 1572872 | tf_op jit(solution)/shard_map/ppermute | solution.py:30
  87.7 17.0 %collective-permute-start.13 = (f32[256,512]{1,0:T(8,128)S(1)}, f32[256,512]{1,0:T(8,128)S(1)}, u32[]{:S(2)}, u32[]{:S(2)}) collective-permute-start(f32[256,512]{1,0:T(8,128)S(1)} %get-tuple-element.12.top), channel_id=1, source_target_pairs={{0,96},{32,0},{64,32},{96,64},{1,97},{33,1},{65,33},{97,65},{2,98}... | collective-permute-start | bytes 1572872 | tf_op jit(solution)/shard_map/ppermute | solution.py:30
  94.6 9.6 %collective-permute-start.16 = (f32[64,1024]{1,0:T(8,128)S(1)}, f32[64,1024]{1,0:T(8,128)S(1)}, u32[]{:S(2)}, u32[]{:S(2)}) collective-permute-start(f32[64,1024]{1,0:T(8,128)S(1)} %slice.46), channel_id=1, source_target_pairs={{0,8},{1,9},{2,10},{3,11},{4,12},{5,13},{6,14},{7,15},{8,16},{9,17... | collective-permute-start | bytes 786440 | tf_op jit(solution)/shard_map/ppermute | solution.py:210
  97.3 7.5 %collective-permute-start.17 = (f32[64,1024]{1,0:T(8,128)S(1)}, f32[64,1024]{1,0:T(8,128)S(1)}, u32[]{:S(2)}, u32[]{:S(2)}) collective-permute-start(f32[64,1024]{1,0:T(8,128)S(1)} %slice.47), channel_id=1, source_target_pairs={{0,24},{1,25},{2,26},{3,27},{4,28},{5,29},{6,30},{7,31},{8,0},{9,1... | collective-permute-start | bytes 786440 | tf_op jit(solution)/shard_map/ppermute | solution.py:210

commit v4 on v3

--- a/solution.py
+++ b/solution.py
@@ -57,10 +57,9 @@
         lo[rows, place] = l
 
 
-def place_left(pieces, hi, lo):
+def place_left(placed, hi, lo):
     z = lax.axis_index("col") // 8
-    own, up, down, far_first, far_second = pieces
-    for by, at, source in ((0, 0, own), (3, 0, up), (1, 0, down), (2, 0, far_first), (2, 64, far_second)):
+    for by, at, source in placed:
         size = source.shape[0]
         rows = pl.ds(pl.multiple_of((z + by) % 4 * 128 + at, size), size)
         h, l = split(source[...])
@@ -83,16 +82,25 @@
         mr[t, :] = m[:, HALF:]
 
 
-def middle(ml, mr, hl, hr, own, core, next_own, next_core, p0, p1, p2, p3, p4, *rest):
-    top, mid, low, x, qh, ql, lh, ll = rest[-8:]
+def prepare(ml, mr, own, core, next_own, next_core, p0, p1, p2, x, ah, al, lh, ll, qh, ql):
     place_right(own, core, slice(WIN, WIN + HALF), slice(0, HALF), qh, ql)
     place_right(next_own, next_core, slice(0, HALF), slice(HALF, WIN), qh, ql)
-    for c, (u, v) in enumerate(((hl, ml), (mr, hr))):
+    first, second = slice(0, HALF), slice(HALF, WIN)
+    x[:, first] = dot3(split(ml[...]), (qh[second, first], ql[second, first]), NN)
+    x[:, second] = dot3(split(mr[...]), (qh[first, second], ql[first, second]), NN)
+    for to, part in ((ah, qh), (al, ql)):
+        to[:, first] = part[first, first]
+        to[:, second] = part[second, second]
+    place_left(((0, 0, p0), (3, 0, p1), (1, 0, p2)), lh, ll)
+
+
+def middle(hl, hr, own, ah, al, near_h, near_l, p3, p4, top, mid, low, x, lh, ll):
+    lh[...] = near_h[...]
+    ll[...] = near_l[...]
+    place_left(((2, 0, p3), (2, 64, p4)), lh, ll)
+    for c, u in enumerate((hl, hr)):
         cols = slice(c * HALF, (c + 1) * HALF)
-        first = (qh[:HALF, cols], ql[:HALF, cols])
-        second = (qh[HALF:, cols], ql[HALF:, cols])
-        x[:, cols] = dot3(split(u[...]), first, NN) + dot3(split(v[...]), second, NN)
-    place_left((p0, p1, p2, p3, p4), lh, ll)
+        x[:, cols] = own[:, cols] + dot3(split(u[...]), (ah[:, cols], al[:, cols]), NN)
     for k in range(2):
         cols = slice(k * WIN, (k + 1) * WIN)
         n = dot3((lh[:, cols], ll[:, cols]), split(x[cols, :]), TN)
@@ -105,7 +113,7 @@
 
 
 def left_shifted(top, mid, low, above, below, p0, p1, p2, p3, p4, out, y, qh, ql, sems):
-    place_left((p0, p1, p2, p3, p4), qh, ql)
+    place_left(((0, 0, p0), (3, 0, p1), (1, 0, p2), (2, 0, p3), (2, 64, p4)), qh, ql)
 
     def q(rows, cols):
         return qh[rows, cols], ql[rows, cols]
@@ -174,13 +182,25 @@
     return call(right_aligned, [half, half], (schur, *pieces, *after), specs, scratch, FLOPS, 5, 12)
 
 
-def middle_products(parts, r2, l1, after):
-    args = (*parts, *r2, *l1)
-    scratch = [pltpu.VMEM((2 * WIN, WIN), F32)]
-    scratch += [pltpu.VMEM((WIN, WIN), BF16)] * 2 + [pltpu.VMEM((WIN, 2 * WIN), BF16)] * 2
+def prepared(parts, r2, near):
+    args = (*parts, *r2, *near)
+    outs = [((2 * WIN, WIN), F32)] + [((HALF, WIN), BF16)] * 2 + [((WIN, 2 * WIN), BF16)] * 2
+    return pl.pallas_call(
+        prepare,
+        out_shape=tuple(jax.ShapeDtypeStruct(*o) for o in outs),
+        in_specs=[VMEM] * len(args),
+        out_specs=(VMEM,) * len(outs),
+        scratch_shapes=[pltpu.VMEM((WIN, WIN), BF16)] * 2,
+        compiler_params=pltpu.CompilerParams(vmem_limit_bytes=16 * 2**20),
+        cost_estimate=pl.CostEstimate(flops=FLOPS // 2, bytes_accessed=7 * 2**20, transcendentals=0),
+    )(*args)
+
+
+def middle_products(parts, ready, far):
+    args = (*parts, *ready, *far)
+    scratch = [pltpu.VMEM((2 * WIN, WIN), F32)] + [pltpu.VMEM((WIN, 2 * WIN), BF16)] * 2
     outs = [(HALF, WIN), (WIN, WIN), (HALF, WIN)]
-    specs = [VMEM] * len(args) + [ANY] * len(after)
-    return call(middle, outs, (*args, *after), specs, scratch, 2 * FLOPS, 9, 20)
+    return call(middle, outs, args, [VMEM] * len(args), scratch, 3 * FLOPS // 2, 9, 20)
 
 
 def last_left(parts, l2):
@@ -222,7 +242,7 @@
 
 def body(schur, left_rot, right_rot, left_off, right_off):
     l1 = gathered(jnp.concatenate([left_rot[0], left_rot[1]], axis=1))
-    l1 = around(l1, along_z)
+    l1 = l1, ring(l1, along_z(1)), ring(l1, along_z(-1))
     right_next = right_off[0, :, :HALF]
     right_next = stacked([shift(right_next, "col", -1), across_next(right_next)])
     away = shift(left_off[0, :, :HALF], "row", -1)
@@ -244,9 +264,15 @@
     hl = shift(mr, "col", 1)
     hr = shift(ml, "col", -1)
     next_core = swap(right_next, "row", 1)
-    top, mid, low = middle_products(
-        (ml, mr, hl, hr), (right, right_core, right_next, next_core), l1, ()
+    ready = prepared((ml, mr), (right, right_core, right_next, next_core), l1[:3])
+    far_first, far_second = joined(
+        [(64, 2 * WIN)] * 2,
+        [l1[1], l1[2]],
+        [(k, (slice(k * 64, k * 64 + 64), EVERY), k, (EVERY, EVERY)) for k in (0, 1)],
+        after=(ready[0],),
     )
+    far = ring(far_first, along_z(1)), ring(far_second, along_z(-1))
+    top, mid, low = middle_products((hl, hr), ready, far)
     l2 = around(l2, along_z)
     above = shift(low, "row", 1)
     below = shift(top, "row", -1)

time: 108 us -> 108 us (level)
    ppermute x8, waiting for transfers between devices: 36.4 us -> 34.6 us  [ring(): return lax.ppermute(x, 'col', perm)]
    ppermute x3, waiting for transfers between devices: 0.01 us -> 1.54 us  [swap(): return lax.ppermute(x, axis, xor_perm(axis, mask))]
    pallas_call x0 -> x1, Pallas kernels: none -> 1.52 us  [prepared(): pl.pallas_call(prepare, out_shape=tuple((jax.ShapeDtypeStruct(*o) for o i...]
    pallas_call x6 -> x7, Pallas kernels: 10.1 us -> 8.87 us  [call(): pl.pallas_call(kernel, out_shape=tuple((jax.ShapeDtypeStruct(s, F32) for...]
  transfers between devices with their start and end apart: 19 -> 19, of which waited for: 6 -> 7; matrix products, arithmetic and copies ran while one was open for 2% -> 2% of each run, Pallas kernels for 4% -> 4%
where the time goes in v4:
time: 108 us
  starting transfers between devices  38.4 us (36%)
  waiting for transfers between devices  37.8 us (35%)
  blocking collectives  17.2 us (16%)
  Pallas kernels  10.4 us (10%)
  local copies, waits for them, and re-layouts  2.74 us (3%)
    ppermute x8, waiting for transfers between devices, ring(): return lax.ppermute(x, 'col', perm)  34.6 us
    ppermute x6, starting transfers between devices, shift(): return lax.ppermute(x, axis, shift_perm(axis, by))  18.7 us
    all_to_all x1, blocking collectives, gathered(): out = lax.all_to_all(copies, 'col', 0, 0, axis_index_groups=groups)  17.2 us
    ppermute x8, starting transfers between devices, ring(): return lax.ppermute(x, 'col', perm)  10.6 us
    pallas_call x7, Pallas kernels, call(): pl.pallas_call(kernel, out_shape=tuple((jax.ShapeDtypeStruct(s, F32) for...  8.87 us
    all_to_all x1, starting transfers between devices, gathered(): out = lax.all_to_all(copies, 'col', 0, 0, axis_index_groups=groups)  6.64 us
    ppermute x3, starting transfers between devices, swap(): return lax.ppermute(x, axis, xor_perm(axis, mask))  2.22 us
  transfers between devices with their start and end apart: 19, of which 7 were waited for; matrix products, arithmetic and copies ran while one was open for 2% of the time, Pallas kernels for 4%

profile of v4, /device:TPU:0, one launch (start us, length us, event | category | flops | bytes accessed | tf_op | source)
XLA Modules:
  0.0 107.7 jit_solution(940574734400271632)
XLA Ops:
  0.0 1.0 slice_bitcast_fusion
  1.0 1.0 pad_maximum_fusion.refs_0_
  2.0 1.7 %collective-permute-start = (f32[128,768]{1,0:T(8,128)S(1)}, f32[128,768]{1,0:T(8,128)S(1)}, u32[]{:S(2)}, u32[]{:S(2)}) collective-permute-start(f32[128,768]{1,0:T(8,128)S(1)} %pad_maximum_fusion.refs_0_), channel_id=1, source_target_pairs={{0,64},{32,96},{64,0},{96,32},{1,65},{33,97},{65,1},{97,33},{2,66}... | collective-permute-start | bytes 1179656 | tf_op jit(solution)/shard_map/ppermute | solution.py:26
  3.7 0.8 slice_bitcast_fusion.3
  4.4 0.8 broadcast_in_dim.5
  5.3 6.6 %all-to-all-start.1 = ((f32[8,16,1024]{2,1,0:T(8,128)}), f32[8,16,1024]{2,1,0:T(8,128)S(1)}, u32[]{:S(2)}, u32[]{:S(2)}) async-start(f32[8,16,1024]{2,1,0:T(8,128)} %broadcast_in_dim.5), calls=%async_computation.1 | async-start | bytes 1048576 | tf_op jit(solution)/shard_map/all_to_all | solution.py:224
  11.9 9.1 %collective-permute-start.3 = (f32[128,256]{1,0:T(8,128)S(1)}, f32[128,256]{1,0:T(8,128)S(1)}, u32[]{:S(2)}, u32[]{:S(2)}) collective-permute-start(f32[128,256]{1,0:T(8,128)S(1)} %get-tuple-element.29), channel_id=1, source_target_pairs={{0,31},{1,0},{2,1},{3,2},{4,3},{5,4},{6,5},{7,6},{8,7},{9,8},{10,9... | collective-permute-start | bytes 393224 | tf_op jit(solution)/shard_map/ppermute | solution.py:30
  21.0 0.2 collective-permute-start.4
  21.3 0.1 shard_map.55.own
  21.4 0.6 collective-permute-start.1
  21.9 1.7 %all-to-all-done.1 = f32[8,16,1024]{2,1,0:T(8,128)S(1)} async-done(((f32[8,16,1024]{2,1,0:T(8,128)}), f32[8,16,1024]{2,1,0:T(8,128)S(1)}, u32[]{:S(2)}, u32[]{:S(2)}) %all-to-all-start.1) | async-done | bytes 524320 | tf_op jit(solution)/shard_map/all_to_all | solution.py:224
  23.6 1.9 %collective-permute-start.5 = (f32[128,1024]{1,0:T(8,128)S(1)}, f32[128,1024]{1,0:T(8,128)S(1)}, u32[]{:S(2)}, u32[]{:S(2)}) collective-permute-start(f32[128,1024]{1,0:T(8,128)S(1)} %bitcast.21), channel_id=1, source_target_pairs={{0,8},{1,9},{2,10},{3,11},{4,12},{5,13},{6,14},{7,15},{8,16},{9,17... | collective-permute-start | bytes 1572872 | tf_op jit(solution)/shard_map/ppermute | solution.py:230
  25.5 3.8 %collective-permute-start.6 = (f32[128,1024]{1,0:T(8,128)S(1)}, f32[128,1024]{1,0:T(8,128)S(1)}, u32[]{:S(2)}, u32[]{:S(2)}) collective-permute-start(f32[128,1024]{1,0:T(8,128)S(1)} %bitcast.22), channel_id=1, source_target_pairs={{0,24},{1,25},{2,26},{3,27},{4,28},{5,29},{6,30},{7,31},{8,0},{9,1... | collective-permute-start | bytes 1572872 | tf_op jit(solution)/shard_map/ppermute | solution.py:230
  29.4 17.2 %all_to_all.10 = f32[8,16,1024]{2,1,0:T(8,128)S(1)} all-to-all(f32[8,16,1024]{2,1,0:T(8,128)S(1)} %broadcast_in_dim.4), channel_id=1, replica_groups={{0,1,2,3,4,5,6,7},{8,9,10,11,12,13,14,15},{16,17,18,19,20,21,22,23},{24..., dimensions={0} | all-to-all | bytes 1048576 | tf_op jit(solution)/shard_map/all_to_all | solution.py:224
  46.6 2.7 %shard_map.58 = (f32[1024,256]{1,0:T(8,128)S(1)}, f32[1024,256]{1,0:T(8,128)S(1)}) custom-call(f32[1024,512]{1,0:T(8,128)S(1)} %copy-done, f32[256,768]{1,0:T(8,128)S(1)} %shard_map.55.own, f32[256,768]{1,0:T(8,128)S(1)} %collective-permute-done.1.core, f32[128,1024]{1,0:T(8,128)S(1)} %bitcast.17, f32[128,1024]{1,0:T(8,128)S(1)} %collective-permute-done.5.rest_1_.p1.refs_0_, ...), custom_call_target="tpu_custom_call" | custom-call | flops 1610612736 | bytes 5242880 | tf_op jit(solution)/shard_map/pallas_call | solution.py:147
  49.3 0.3 collective-permute-start.7
  49.6 7.5 %collective-permute-start.8 = (f32[1024,256]{1,0:T(8,128)S(1)}, f32[1024,256]{1,0:T(8,128)S(1)}, u32[]{:S(2)}, u32[]{:S(2)}) collective-permute-start(f32[1024,256]{1,0:T(8,128)S(1)} %get-tuple-element.18.ml), channel_id=1, source_target_pairs={{0,31},{1,0},{2,1},{3,2},{4,3},{5,4},{6,5},{7,6},{8,7},{9,8},{10,9... | collective-permute-start | bytes 3145736 | tf_op jit(solution)/shard_map/ppermute | solution.py:30
  57.1 1.5 %collective-permute-done.9.next_core = f32[256,256]{1,0:T(8,128)S(1)} collective-permute-done((f32[256,256]{1,0:T(8,128)S(1)}, f32[256,256]{1,0:T(8,128)S(1)}, u32[]{:S(2)}, u32[]{:S(2)}) %collective-permute-start.9) | collective-permute-done | bytes 262176 | tf_op jit(solution)/shard_map/ppermute | solution.py:26
  58.7 1.5 %shard_map.59 = (f32[1024,512]{1,0:T(8,128)S(1)}, bf16[256,512]{1,0:T(8,128)(2,1)S(1)}, bf16[256,512]{1,0:T(8,128)(2,1)S(1)}, bf16[512,1024]{1,0:T(8,128)(2,1)S(1)}, bf16[512,1024]{1,0:T(8,128)(2,1)S(1)}) custom-call(f32[1024,256]{1,0:T(8,128)S(1)} %get-tuple-element.18.ml, f32[1024,256]{1,0:T(8,128)S(1)} %get-tuple-element.17.mr, ...), custom_call_target="tpu_custom_call" | custom-call | flops 805306368 | bytes 7340032 | tf_op jit(solution)/shard_map/pallas_call | solution.py:188
  60.2 0.1 collective-permute-start.10
  60.3 3.2 %collective-permute-start.11 = (f32[64,1024]{1,0:T(8,128)S(1)}, f32[64,1024]{1,0:T(8,128)S(1)}, u32[]{:S(2)}, u32[]{:S(2)}) collective-permute-start(f32[64,1024]{1,0:T(8,128)S(1)} %get-tuple-element.25), channel_id=1, source_target_pairs={{0,24},{1,25},{2,26},{3,27},{4,28},{5,29},{6,30},{7,31},{8,0},{9,1... | collective-permute-start | bytes 786440 | tf_op jit(solution)/shard_map/ppermute | solution.py:230
  63.6 19.9 %collective-permute-done.10.p3 = f32[64,1024]{1,0:T(8,128)S(1)} collective-permute-done((f32[64,1024]{1,0:T(8,128)S(1)}, f32[64,1024]{1,0:T(8,128)S(1)}, u32[]{:S(2)}, u32[]{:S(2)}) %collective-permute-start.10) | collective-permute-done | bytes 262176 | tf_op jit(solution)/shard_map/ppermute | solution.py:230
  83.4 2.9 %shard_map.61 = (f32[256,512]{1,0:T(8,128)S(1)}, f32[512,512]{1,0:T(8,128)S(1)}, f32[256,512]{1,0:T(8,128)S(1)}) custom-call(f32[1024,256]{1,0:T(8,128)S(1)} %collective-permute-done.7.hl, f32[1024,256]{1,0:T(8,128)S(1)} %collective-permute-done.8.hr, f32[1024,512]{1,0:T(8,128)S(1)} %get-tuple-element.19.refs_2_.own, ...), custom_call_target="tpu_custom_call" | custom-call | flops 2415919104 | bytes 9437184 | tf_op jit(solution)/shard_map/pallas_call | solution.py:147
  86.4 0.1 collective-permute-start.12
  86.5 1.7 %collective-permute-start.13 = (f32[256,512]{1,0:T(8,128)S(1)}, f32[256,512]{1,0:T(8,128)S(1)}, u32[]{:S(2)}, u32[]{:S(2)}) collective-permute-start(f32[256,512]{1,0:T(8,128)S(1)} %get-tuple-element.26.top), channel_id=1, source_target_pairs={{0,96},{32,0},{64,32},{96,64},{1,97},{33,1},{65,33},{97,65},{2,98}... | collective-permute-start | bytes 1572872 | tf_op jit(solution)/shard_map/ppermute | solution.py:30
  88.2 6.4 %collective-permute-done.14.p1 = f32[128,1024]{1,0:T(8,128)S(1)} collective-permute-done((f32[128,1024]{1,0:T(8,128)S(1)}, f32[128,1024]{1,0:T(8,128)S(1)}, u32[]{:S(2)}, u32[]{:S(2)}) %collective-permute-start.14) | collective-permute-done | bytes 524320 | tf_op jit(solution)/shard_map/ppermute | solution.py:230
  94.6 0.1 collective-permute-start.16
  94.7 2.5 %collective-permute-done.15.p2 = f32[128,1024]{1,0:T(8,128)S(1)} collective-permute-done((f32[128,1024]{1,0:T(8,128)S(1)}, f32[128,1024]{1,0:T(8,128)S(1)}, u32[]{:S(2)}, u32[]{:S(2)}) %collective-permute-start.15) | collective-permute-done | bytes 524320 | tf_op jit(solution)/shard_map/ppermute | solution.py:230
  97.2 1.6 %collective-permute-start.17 = (f32[64,1024]{1,0:T(8,128)S(1)}, f32[64,1024]{1,0:T(8,128)S(1)}, u32[]{:S(2)}, u32[]{:S(2)}) collective-permute-start(f32[64,1024]{1,0:T(8,128)S(1)} %slice.37), channel_id=1, source_target_pairs={{0,24},{1,25},{2,26},{3,27},{4,28},{5,29},{6,30},{7,31},{8,0},{9,1... | collective-permute-start | bytes 786440 | tf_op jit(solution)/shard_map/ppermute | solution.py:230
  98.8 5.3 %collective-permute-done.16.p3 = f32[64,1024]{1,0:T(8,128)S(1)} collective-permute-done((f32[64,1024]{1,0:T(8,128)S(1)}, f32[64,1024]{1,0:T(8,128)S(1)}, u32[]{:S(2)}, u32[]{:S(2)}) %collective-permute-start.16) | collective-permute-done | bytes 262176 | tf_op jit(solution)/shard_map/ppermute | solution.py:230
  104.1 0.5 collective-permute-done.17.p4
  104.6 3.1 %shard_map.62 = f32[1024,512]{1,0:T(8,128)} custom-call(f32[256,512]{1,0:T(8,128)S(1)} %get-tuple-element.26.top, f32[512,512]{1,0:T(8,128)S(1)} %get-tuple-element.27.mid, f32[256,512]{1,0:T(8,128)S(1)} %get-tuple-element.28.low, f32[256,512]{1,0:T(8,128)S(1)} %collective-permute-done.12.above, f32[256,512]{1,0:T(8,128)S(1)} %collective-permute-done.13.below, ...), custom_call_target="tpu_custom_call" | custom-call | flops 1610612736 | bytes 7340032 | tf_op jit(solution)/shard_map/pallas_call | solution.py:147
  (30 shorter events, 0.2 us)
Async XLA Ops:
  0.0 21.3 %copy-start.1 = (f32[2,16,512]{2,1,0:T(8,128)S(1)}, f32[2,16,512]{2,1,0:T(8,128)}, u32[]{:S(2)}) copy-start(f32[2,16,512]{2,1,0:T(8,128)} %param.8) | copy-start | bytes 196612
  2.0 19.3 %collective-permute-start = (f32[128,768]{1,0:T(8,128)S(1)}, f32[128,768]{1,0:T(8,128)S(1)}, u32[]{:S(2)}, u32[]{:S(2)}) collective-permute-start(f32[128,768]{1,0:T(8,128)S(1)} %pad_maximum_fusion.refs_0_), channel_id=1, source_target_pairs={{0,64},{32,96},{64,0},{96,32},{1,65},{33,97},{65,1},{97,33},{2,66}... | collective-permute-start | bytes 1179656 | tf_op jit(solution)/shard_map/ppermute | solution.py:26
  5.3 18.3 %all-to-all-start.1 = ((f32[8,16,1024]{2,1,0:T(8,128)}), f32[8,16,1024]{2,1,0:T(8,128)S(1)}, u32[]{:S(2)}, u32[]{:S(2)}) async-start(f32[8,16,1024]{2,1,0:T(8,128)} %broadcast_in_dim.5), calls=%async_computation.1 | async-start | bytes 1048576 | tf_op jit(solution)/shard_map/all_to_all | solution.py:224
  11.9 13.6 %collective-permute-start.3 = (f32[128,256]{1,0:T(8,128)S(1)}, f32[128,256]{1,0:T(8,128)S(1)}, u32[]{:S(2)}, u32[]{:S(2)}) collective-permute-start(f32[128,256]{1,0:T(8,128)S(1)} %get-tuple-element.29), channel_id=1, source_target_pairs={{0,31},{1,0},{2,1},{3,2},{4,3},{5,4},{6,5},{7,6},{8,7},{9,8},{10,9... | collective-permute-start | bytes 393224 | tf_op jit(solution)/shard_map/ppermute | solution.py:30
  21.0 8.2 %collective-permute-start.4 = (f32[128,256]{1,0:T(8,128)S(1)}, f32[128,256]{1,0:T(8,128)S(1)}, u32[]{:S(2)}, u32[]{:S(2)}) collective-permute-start(f32[128,256]{1,0:T(8,128)S(1)} %get-tuple-element.29), channel_id=1, source_target_pairs={{0,95},{1,64},{2,65},{3,66},{4,67},{5,68},{6,69},{7,70},{8,71},{9,... | collective-permute-start | bytes 393224 | tf_op jit(solution)/shard_map/ppermute | solution.py:217
  21.3 8.0 %collective-permute-start.2 = (f32[16,256]{1,0:T(8,128)S(1)}, f32[16,256]{1,0:T(8,128)S(1)}, u32[]{:S(2)}, u32[]{:S(2)}) collective-permute-start(f32[16,256]{1,0:T(8,128)S(1)} %get-tuple-element.33), channel_id=1, source_target_pairs={{0,96},{32,0},{64,32},{96,64},{1,97},{33,1},{65,33},{97,65},{2,98}... | collective-permute-start | bytes 49160 | tf_op jit(solution)/shard_map/ppermute | solution.py:30
  21.4 25.3 %collective-permute-start.1 = (f32[256,768]{1,0:T(8,128)S(1)}, f32[256,768]{1,0:T(8,128)S(1)}, u32[]{:S(2)}, u32[]{:S(2)}) collective-permute-start(f32[256,768]{1,0:T(8,128)S(1)} %shard_map.55.own), channel_id=1, source_target_pairs={{0,32},{32,0},{64,96},{96,64},{1,33},{33,1},{65,97},{97,65},{2,34}... | collective-permute-start | bytes 2359304 | tf_op jit(solution)/shard_map/ppermute | solution.py:26
  23.6 23.0 %copy-start = (f32[1024,512]{1,0:T(8,128)S(1)}, f32[1024,512]{1,0:T(8,128)}, u32[]{:S(2)}) copy-start(f32[1024,512]{1,0:T(8,128)} %s.1) | copy-start | bytes 6291460
  23.6 23.0 %collective-permute-start.5 = (f32[128,1024]{1,0:T(8,128)S(1)}, f32[128,1024]{1,0:T(8,128)S(1)}, u32[]{:S(2)}, u32[]{:S(2)}) collective-permute-start(f32[128,1024]{1,0:T(8,128)S(1)} %bitcast.21), channel_id=1, source_target_pairs={{0,8},{1,9},{2,10},{3,11},{4,12},{5,13},{6,14},{7,15},{8,16},{9,17... | collective-permute-start | bytes 1572872 | tf_op jit(solution)/shard_map/ppermute | solution.py:230
  25.5 21.1 %collective-permute-start.6 = (f32[128,1024]{1,0:T(8,128)S(1)}, f32[128,1024]{1,0:T(8,128)S(1)}, u32[]{:S(2)}, u32[]{:S(2)}) collective-permute-start(f32[128,1024]{1,0:T(8,128)S(1)} %bitcast.22), channel_id=1, source_target_pairs={{0,24},{1,25},{2,26},{3,27},{4,28},{5,29},{6,30},{7,31},{8,0},{9,1... | collective-permute-start | bytes 1572872 | tf_op jit(solution)/shard_map/ppermute | solution.py:230
  49.3 34.1 %collective-permute-start.7 = (f32[1024,256]{1,0:T(8,128)S(1)}, f32[1024,256]{1,0:T(8,128)S(1)}, u32[]{:S(2)}, u32[]{:S(2)}) collective-permute-start(f32[1024,256]{1,0:T(8,128)S(1)} %get-tuple-element.17.mr), channel_id=1, source_target_pairs={{0,1},{1,2},{2,3},{3,4},{4,5},{5,6},{6,7},{7,8},{8,9},{9,10},{10,1... | collective-permute-start | bytes 3145736 | tf_op jit(solution)/shard_map/ppermute | solution.py:30
  49.6 33.8 %collective-permute-start.8 = (f32[1024,256]{1,0:T(8,128)S(1)}, f32[1024,256]{1,0:T(8,128)S(1)}, u32[]{:S(2)}, u32[]{:S(2)}) collective-permute-start(f32[1024,256]{1,0:T(8,128)S(1)} %get-tuple-element.18.ml), channel_id=1, source_target_pairs={{0,31},{1,0},{2,1},{3,2},{4,3},{5,4},{6,5},{7,6},{8,7},{9,8},{10,9... | collective-permute-start | bytes 3145736 | tf_op jit(solution)/shard_map/ppermute | solution.py:30
  57.1 1.5 %collective-permute-start.9 = (f32[256,256]{1,0:T(8,128)S(1)}, f32[256,256]{1,0:T(8,128)S(1)}, u32[]{:S(2)}, u32[]{:S(2)}) collective-permute-start(f32[256,256]{1,0:T(8,128)S(1)} %shard_map.56.refs_2_.next_own), channel_id=1, source_target_pairs={{0,32},{32,0},{64,96},{96,64},{1,33},{33,1},{65,97},{97,65},{2,34}... | collective-permute-start | bytes 786440 | tf_op jit(solution)/shard_map/ppermute | solution.py:26
  60.2 23.2 %collective-permute-start.10 = (f32[64,1024]{1,0:T(8,128)S(1)}, f32[64,1024]{1,0:T(8,128)S(1)}, u32[]{:S(2)}, u32[]{:S(2)}) collective-permute-start(f32[64,1024]{1,0:T(8,128)S(1)} %get-tuple-element.24), channel_id=1, source_target_pairs={{0,8},{1,9},{2,10},{3,11},{4,12},{5,13},{6,14},{7,15},{8,16},{9,17... | collective-permute-start | bytes 786440 | tf_op jit(solution)/shard_map/ppermute | solution.py:230
  60.3 23.1 %collective-permute-start.11 = (f32[64,1024]{1,0:T(8,128)S(1)}, f32[64,1024]{1,0:T(8,128)S(1)}, u32[]{:S(2)}, u32[]{:S(2)}) collective-permute-start(f32[64,1024]{1,0:T(8,128)S(1)} %get-tuple-element.25), channel_id=1, source_target_pairs={{0,24},{1,25},{2,26},{3,27},{4,28},{5,29},{6,30},{7,31},{8,0},{9,1... | collective-permute-start | bytes 786440 | tf_op jit(solution)/shard_map/ppermute | solution.py:230
  63.6 31.0 %collective-permute-start.14 = (f32[128,1024]{1,0:T(8,128)S(1)}, f32[128,1024]{1,0:T(8,128)S(1)}, u32[]{:S(2)}, u32[]{:S(2)}) collective-permute-start(f32[128,1024]{1,0:T(8,128)S(1)} %bitcast.18), channel_id=1, source_target_pairs={{0,8},{1,9},{2,10},{3,11},{4,12},{5,13},{6,14},{7,15},{8,16},{9,17... | collective-permute-start | bytes 1572872 | tf_op jit(solution)/shard_map/ppermute | solution.py:230
  83.4 13.8 %collective-permute-start.15 = (f32[128,1024]{1,0:T(8,128)S(1)}, f32[128,1024]{1,0:T(8,128)S(1)}, u32[]{:S(2)}, u32[]{:S(2)}) collective-permute-start(f32[128,1024]{1,0:T(8,128)S(1)} %bitcast.19), channel_id=1, source_target_pairs={{0,24},{1,25},{2,26},{3,27},{4,28},{5,29},{6,30},{7,31},{8,0},{9,1... | collective-permute-start | bytes 1572872 | tf_op jit(solution)/shard_map/ppermute | solution.py:230
  86.4 18.2 %collective-permute-start.12 = (f32[256,512]{1,0:T(8,128)S(1)}, f32[256,512]{1,0:T(8,128)S(1)}, u32[]{:S(2)}, u32[]{:S(2)}) collective-permute-start(f32[256,512]{1,0:T(8,128)S(1)} %get-tuple-element.28.low), channel_id=1, source_target_pairs={{0,32},{32,64},{64,96},{96,0},{1,33},{33,65},{65,97},{97,1},{2,34}... | collective-permute-start | bytes 1572872 | tf_op jit(solution)/shard_map/ppermute | solution.py:30
  86.5 18.1 %collective-permute-start.13 = (f32[256,512]{1,0:T(8,128)S(1)}, f32[256,512]{1,0:T(8,128)S(1)}, u32[]{:S(2)}, u32[]{:S(2)}) collective-permute-start(f32[256,512]{1,0:T(8,128)S(1)} %get-tuple-element.26.top), channel_id=1, source_target_pairs={{0,96},{32,0},{64,32},{96,64},{1,97},{33,1},{65,33},{97,65},{2,98}... | collective-permute-start | bytes 1572872 | tf_op jit(solution)/shard_map/ppermute | solution.py:30
  94.6 9.5 %collective-permute-start.16 = (f32[64,1024]{1,0:T(8,128)S(1)}, f32[64,1024]{1,0:T(8,128)S(1)}, u32[]{:S(2)}, u32[]{:S(2)}) collective-permute-start(f32[64,1024]{1,0:T(8,128)S(1)} %slice.36), channel_id=1, source_target_pairs={{0,8},{1,9},{2,10},{3,11},{4,12},{5,13},{6,14},{7,15},{8,16},{9,17... | collective-permute-start | bytes 786440 | tf_op jit(solution)/shard_map/ppermute | solution.py:230
  97.2 7.4 %collective-permute-start.17 = (f32[64,1024]{1,0:T(8,128)S(1)}, f32[64,1024]{1,0:T(8,128)S(1)}, u32[]{:S(2)}, u32[]{:S(2)}) collective-permute-start(f32[64,1024]{1,0:T(8,128)S(1)} %slice.37), channel_id=1, source_target_pairs={{0,24},{1,25},{2,26},{3,27},{4,28},{5,29},{6,30},{7,31},{8,0},{9,1... | collective-permute-start | bytes 786440 | tf_op jit(solution)/shard_map/ppermute | solution.py:230

commit v5 on v4

--- a/solution.py
+++ b/solution.py
@@ -94,25 +94,20 @@
     place_left(((0, 0, p0), (3, 0, p1), (1, 0, p2)), lh, ll)
 
 
-def middle(hl, hr, own, ah, al, near_h, near_l, p3, p4, top, mid, low, x, lh, ll):
-    lh[...] = near_h[...]
-    ll[...] = near_l[...]
-    place_left(((2, 0, p3), (2, 64, p4)), lh, ll)
+def middle(w, hl, hr, own, ah, al, near_h, near_l, p3, p4, first, second, x, lh, ll):
+    window = slice(w * WIN, (w + 1) * WIN)
+    lh[...] = near_h[:, window]
+    ll[...] = near_l[:, window]
+    place_left(((2, 0, p3.at[:, window]), (2, 64, p4.at[:, window])), lh, ll)
     for c, u in enumerate((hl, hr)):
         cols = slice(c * HALF, (c + 1) * HALF)
-        x[:, cols] = own[:, cols] + dot3(split(u[...]), (ah[:, cols], al[:, cols]), NN)
-    for k in range(2):
-        cols = slice(k * WIN, (k + 1) * WIN)
-        n = dot3((lh[:, cols], ll[:, cols]), split(x[cols, :]), TN)
-        if k == 0:
-            top[...] = n[:HALF]
-            mid[:HALF, :] = n[HALF:]
-        else:
-            mid[HALF:, :] = n[:HALF]
-            low[...] = n[HALF:]
-
-
-def left_shifted(top, mid, low, above, below, p0, p1, p2, p3, p4, out, y, qh, ql, sems):
+        x[:, cols] = own[window, cols] + dot3(split(u[window, :]), (ah[:, cols], al[:, cols]), NN)
+    n = dot3((lh[...], ll[...]), split(x[...]), TN)
+    first[...] = n[:HALF]
+    second[...] = n[HALF:]
+
+
+def left_shifted(top, upper, lower, low, above, below, p0, p1, p2, p3, p4, out, y, qh, ql, sems):
     place_left(((0, 0, p0), (3, 0, p1), (1, 0, p2), (2, 0, p3), (2, 64, p4)), qh, ql)
 
     def q(rows, cols):
@@ -125,7 +120,7 @@
 
     first, second = slice(0, HALF), slice(HALF, WIN)
     a, b, c = slice(0, HALF), slice(HALF, HALF + WIN), slice(HALF + WIN, 2 * WIN)
-    y[b, :] = dot3(q(slice(None), b), split(mid[...]), TN)
+    y[b, :] = dot3(q(first, b), split(upper[...]), TN) + dot3(q(second, b), split(lower[...]), TN)
     writes = [write(b, 0)]
     y[a, :] = dot3(q(first, a), split(above[...]), TN) + dot3(q(second, a), split(top[...]), TN)
     writes.append(write(a, 1))
@@ -196,11 +191,11 @@
     )(*args)
 
 
-def middle_products(parts, ready, far):
+def middle_products(w, parts, ready, far):
     args = (*parts, *ready, *far)
-    scratch = [pltpu.VMEM((2 * WIN, WIN), F32)] + [pltpu.VMEM((WIN, 2 * WIN), BF16)] * 2
-    outs = [(HALF, WIN), (WIN, WIN), (HALF, WIN)]
-    return call(middle, outs, args, [VMEM] * len(args), scratch, 3 * FLOPS // 2, 9, 20)
+    scratch = [pltpu.VMEM((WIN, WIN), F32)] + [pltpu.VMEM((WIN, WIN), BF16)] * 2
+    kernel = functools.partial(middle, w)
+    return call(kernel, [(HALF, WIN)] * 2, args, [VMEM] * len(args), scratch, 3 * FLOPS // 4, 5, 20)
 
 
 def last_left(parts, l2):
@@ -272,11 +267,12 @@
         after=(ready[0],),
     )
     far = ring(far_first, along_z(1)), ring(far_second, along_z(-1))
-    top, mid, low = middle_products((hl, hr), ready, far)
+    top, upper = middle_products(0, (hl, hr), ready, far)
+    lower, low = middle_products(1, (hl, hr), ready, far)
     l2 = around(l2, along_z)
     above = shift(low, "row", 1)
     below = shift(top, "row", -1)
-    return last_left((top, mid, low, above, below), l2)
+    return last_left((top, upper, lower, low, above, below), l2)
 
 
 def solution(mesh):

time: 108 us -> 108 us (level)
    pallas_call x7 -> x8, Pallas kernels: 8.87 us -> 8.95 us  [call(): pl.pallas_call(kernel, out_shape=tuple((jax.ShapeDtypeStruct(s, F32) for...]
where the time goes in v5:
time: 108 us
  starting transfers between devices  38.7 us (36%)
  waiting for transfers between devices  37.5 us (35%)
  blocking collectives  17.2 us (16%)
  Pallas kernels  10.5 us (10%)
  local copies, waits for them, and re-layouts  2.74 us (3%)
    ppermute x8, waiting for transfers between devices, ring(): return lax.ppermute(x, 'col', perm)  34.2 us
    ppermute x6, starting transfers between devices, shift(): return lax.ppermute(x, axis, shift_perm(axis, by))  18.8 us
    all_to_all x1, blocking collectives, gathered(): out = lax.all_to_all(copies, 'col', 0, 0, axis_index_groups=groups)  17.2 us
    ppermute x8, starting transfers between devices, ring(): return lax.ppermute(x, 'col', perm)  10.8 us
    pallas_call x8, Pallas kernels, call(): pl.pallas_call(kernel, out_shape=tuple((jax.ShapeDtypeStruct(s, F32) for...  8.95 us
    all_to_all x1, starting transfers between devices, gathered(): out = lax.all_to_all(copies, 'col', 0, 0, axis_index_groups=groups)  6.64 us
    ppermute x3, starting transfers between devices, swap(): return lax.ppermute(x, axis, xor_perm(axis, mask))  2.22 us
  transfers between devices with their start and end apart: 19, of which 7 were waited for; matrix products, arithmetic and copies ran while one was open for 2% of the time, Pallas kernels for 4%

profile of v5, /device:TPU:0, one launch (start us, length us, event | category | flops | bytes accessed | tf_op | source)
XLA Modules:
  0.0 107.9 jit_solution(12890436640206435805)
XLA Ops:
  0.0 1.0 slice_bitcast_fusion
  1.0 1.0 pad_maximum_fusion.refs_0_
  2.0 1.7 %collective-permute-start = (f32[128,768]{1,0:T(8,128)S(1)}, f32[128,768]{1,0:T(8,128)S(1)}, u32[]{:S(2)}, u32[]{:S(2)}) collective-permute-start(f32[128,768]{1,0:T(8,128)S(1)} %pad_maximum_fusion.refs_0_), channel_id=1, source_target_pairs={{0,64},{32,96},{64,0},{96,32},{1,65},{33,97},{65,1},{97,33},{2,66}... | collective-permute-start | bytes 1179656 | tf_op jit(solution)/shard_map/ppermute | solution.py:26
  3.7 0.8 slice_bitcast_fusion.3
  4.4 0.8 broadcast_in_dim.5
  5.3 6.6 %all-to-all-start.1 = ((f32[8,16,1024]{2,1,0:T(8,128)}), f32[8,16,1024]{2,1,0:T(8,128)S(1)}, u32[]{:S(2)}, u32[]{:S(2)}) async-start(f32[8,16,1024]{2,1,0:T(8,128)} %broadcast_in_dim.5), calls=%async_computation.1 | async-start | bytes 1048576 | tf_op jit(solution)/shard_map/all_to_all | solution.py:219
  11.9 9.1 %collective-permute-start.3 = (f32[128,256]{1,0:T(8,128)S(1)}, f32[128,256]{1,0:T(8,128)S(1)}, u32[]{:S(2)}, u32[]{:S(2)}) collective-permute-start(f32[128,256]{1,0:T(8,128)S(1)} %get-tuple-element.31), channel_id=1, source_target_pairs={{0,31},{1,0},{2,1},{3,2},{4,3},{5,4},{6,5},{7,6},{8,7},{9,8},{10,9... | collective-permute-start | bytes 393224 | tf_op jit(solution)/shard_map/ppermute | solution.py:30
  21.0 0.2 collective-permute-start.4
  21.4 0.6 collective-permute-start.1
  21.9 1.7 %all-to-all-done.1 = f32[8,16,1024]{2,1,0:T(8,128)S(1)} async-done(((f32[8,16,1024]{2,1,0:T(8,128)}), f32[8,16,1024]{2,1,0:T(8,128)S(1)}, u32[]{:S(2)}, u32[]{:S(2)}) %all-to-all-start.1) | async-done | bytes 524320 | tf_op jit(solution)/shard_map/all_to_all | solution.py:219
  23.6 1.9 %collective-permute-start.5 = (f32[128,1024]{1,0:T(8,128)S(1)}, f32[128,1024]{1,0:T(8,128)S(1)}, u32[]{:S(2)}, u32[]{:S(2)}) collective-permute-start(f32[128,1024]{1,0:T(8,128)S(1)} %bitcast.21), channel_id=1, source_target_pairs={{0,8},{1,9},{2,10},{3,11},{4,12},{5,13},{6,14},{7,15},{8,16},{9,17... | collective-permute-start | bytes 1572872 | tf_op jit(solution)/shard_map/ppermute | solution.py:225
  25.5 3.8 %collective-permute-start.6 = (f32[128,1024]{1,0:T(8,128)S(1)}, f32[128,1024]{1,0:T(8,128)S(1)}, u32[]{:S(2)}, u32[]{:S(2)}) collective-permute-start(f32[128,1024]{1,0:T(8,128)S(1)} %bitcast.22), channel_id=1, source_target_pairs={{0,24},{1,25},{2,26},{3,27},{4,28},{5,29},{6,30},{7,31},{8,0},{9,1... | collective-permute-start | bytes 1572872 | tf_op jit(solution)/shard_map/ppermute | solution.py:225
  29.4 17.2 %all_to_all.10 = f32[8,16,1024]{2,1,0:T(8,128)S(1)} all-to-all(f32[8,16,1024]{2,1,0:T(8,128)S(1)} %broadcast_in_dim.4), channel_id=1, replica_groups={{0,1,2,3,4,5,6,7},{8,9,10,11,12,13,14,15},{16,17,18,19,20,21,22,23},{24..., dimensions={0} | all-to-all | bytes 1048576 | tf_op jit(solution)/shard_map/all_to_all | solution.py:219
  46.6 2.7 %shard_map.58 = (f32[1024,256]{1,0:T(8,128)S(1)}, f32[1024,256]{1,0:T(8,128)S(1)}) custom-call(f32[1024,512]{1,0:T(8,128)S(1)} %copy-done, f32[256,768]{1,0:T(8,128)S(1)} %shard_map.55.own, f32[256,768]{1,0:T(8,128)S(1)} %collective-permute-done.1.core, f32[128,1024]{1,0:T(8,128)S(1)} %bitcast.17, f32[128,1024]{1,0:T(8,128)S(1)} %collective-permute-done.5.rest_1_.p1.refs_0_, ...), custom_call_target="tpu_custom_call" | custom-call | flops 1610612736 | bytes 5242880 | tf_op jit(solution)/shard_map/pallas_call | solution.py:142
  49.3 0.3 collective-permute-start.7
  49.6 7.5 %collective-permute-start.8 = (f32[1024,256]{1,0:T(8,128)S(1)}, f32[1024,256]{1,0:T(8,128)S(1)}, u32[]{:S(2)}, u32[]{:S(2)}) collective-permute-start(f32[1024,256]{1,0:T(8,128)S(1)} %get-tuple-element.19.ml), channel_id=1, source_target_pairs={{0,31},{1,0},{2,1},{3,2},{4,3},{5,4},{6,5},{7,6},{8,7},{9,8},{10,9... | collective-permute-start | bytes 3145736 | tf_op jit(solution)/shard_map/ppermute | solution.py:30
  57.2 1.5 %collective-permute-done.9.next_core = f32[256,256]{1,0:T(8,128)S(1)} collective-permute-done((f32[256,256]{1,0:T(8,128)S(1)}, f32[256,256]{1,0:T(8,128)S(1)}, u32[]{:S(2)}, u32[]{:S(2)}) %collective-permute-start.9) | collective-permute-done | bytes 262176 | tf_op jit(solution)/shard_map/ppermute | solution.py:26
  58.7 1.5 %shard_map.59 = (f32[1024,512]{1,0:T(8,128)S(1)}, bf16[256,512]{1,0:T(8,128)(2,1)S(1)}, bf16[256,512]{1,0:T(8,128)(2,1)S(1)}, bf16[512,1024]{1,0:T(8,128)(2,1)S(1)}, bf16[512,1024]{1,0:T(8,128)(2,1)S(1)}) custom-call(f32[1024,256]{1,0:T(8,128)S(1)} %get-tuple-element.19.ml, f32[1024,256]{1,0:T(8,128)S(1)} %get-tuple-element.18.mr, ...), custom_call_target="tpu_custom_call" | custom-call | flops 805306368 | bytes 7340032 | tf_op jit(solution)/shard_map/pallas_call | solution.py:183
  60.3 0.1 collective-permute-start.10
  60.4 3.2 %collective-permute-start.11 = (f32[64,1024]{1,0:T(8,128)S(1)}, f32[64,1024]{1,0:T(8,128)S(1)}, u32[]{:S(2)}, u32[]{:S(2)}) collective-permute-start(f32[64,1024]{1,0:T(8,128)S(1)} %get-tuple-element.26), channel_id=1, source_target_pairs={{0,24},{1,25},{2,26},{3,27},{4,28},{5,29},{6,30},{7,31},{8,0},{9,1... | collective-permute-start | bytes 786440 | tf_op jit(solution)/shard_map/ppermute | solution.py:225
  63.6 19.8 %collective-permute-done.10.p3 = f32[64,1024]{1,0:T(8,128)S(1)} collective-permute-done((f32[64,1024]{1,0:T(8,128)S(1)}, f32[64,1024]{1,0:T(8,128)S(1)}, u32[]{:S(2)}, u32[]{:S(2)}) %collective-permute-start.10) | collective-permute-done | bytes 262176 | tf_op jit(solution)/shard_map/ppermute | solution.py:225
  83.4 1.5 %shard_map.62 = (f32[256,512]{1,0:T(8,128)S(1)}, f32[256,512]{1,0:T(8,128)S(1)}) custom-call(f32[1024,256]{1,0:T(8,128)S(1)} %collective-permute-done.7.hl, f32[1024,256]{1,0:T(8,128)S(1)} %collective-permute-done.8.hr, f32[1024,512]{1,0:T(8,128)S(1)} %get-tuple-element.20.refs_2_.own, bf16[256,512]{1,0:T(8,128)(2,1)S(1)} %get-tuple-element.21.ah, ...), custom_call_target="tpu_custom_call" | custom-call | flops 1207959552 | bytes 5242880 | tf_op jit(solution)/shard_map/pallas_call | solution.py:142
  84.9 0.1 collective-permute-start.12
  85.0 1.5 %shard_map.61 = (f32[256,512]{1,0:T(8,128)S(1)}, f32[256,512]{1,0:T(8,128)S(1)}) custom-call(f32[1024,256]{1,0:T(8,128)S(1)} %collective-permute-done.7.hl, f32[1024,256]{1,0:T(8,128)S(1)} %collective-permute-done.8.hr, f32[1024,512]{1,0:T(8,128)S(1)} %get-tuple-element.20.refs_2_.own, bf16[256,512]{1,0:T(8,128)(2,1)S(1)} %get-tuple-element.21.ah, ...), custom_call_target="tpu_custom_call" | custom-call | flops 1207959552 | bytes 5242880 | tf_op jit(solution)/shard_map/pallas_call | solution.py:142
  86.5 1.8 %collective-permute-start.13 = (f32[256,512]{1,0:T(8,128)S(1)}, f32[256,512]{1,0:T(8,128)S(1)}, u32[]{:S(2)}, u32[]{:S(2)}) collective-permute-start(f32[256,512]{1,0:T(8,128)S(1)} %get-tuple-element.27.top), channel_id=1, source_target_pairs={{0,96},{32,0},{64,32},{96,64},{1,97},{33,1},{65,33},{97,65},{2,98}... | collective-permute-start | bytes 1572872 | tf_op jit(solution)/shard_map/ppermute | solution.py:30
  88.3 6.2 %collective-permute-done.14.p1 = f32[128,1024]{1,0:T(8,128)S(1)} collective-permute-done((f32[128,1024]{1,0:T(8,128)S(1)}, f32[128,1024]{1,0:T(8,128)S(1)}, u32[]{:S(2)}, u32[]{:S(2)}) %collective-permute-start.14) | collective-permute-done | bytes 524320 | tf_op jit(solution)/shard_map/ppermute | solution.py:225
  94.6 0.3 collective-permute-start.16
  94.9 2.3 %collective-permute-done.15.p2 = f32[128,1024]{1,0:T(8,128)S(1)} collective-permute-done((f32[128,1024]{1,0:T(8,128)S(1)}, f32[128,1024]{1,0:T(8,128)S(1)}, u32[]{:S(2)}, u32[]{:S(2)}) %collective-permute-start.15) | collective-permute-done | bytes 524320 | tf_op jit(solution)/shard_map/ppermute | solution.py:225
  97.2 1.6 %collective-permute-start.17 = (f32[64,1024]{1,0:T(8,128)S(1)}, f32[64,1024]{1,0:T(8,128)S(1)}, u32[]{:S(2)}, u32[]{:S(2)}) collective-permute-start(f32[64,1024]{1,0:T(8,128)S(1)} %slice.37), channel_id=1, source_target_pairs={{0,24},{1,25},{2,26},{3,27},{4,28},{5,29},{6,30},{7,31},{8,0},{9,1... | collective-permute-start | bytes 786440 | tf_op jit(solution)/shard_map/ppermute | solution.py:225
  98.8 5.5 %collective-permute-done.16.p3 = f32[64,1024]{1,0:T(8,128)S(1)} collective-permute-done((f32[64,1024]{1,0:T(8,128)S(1)}, f32[64,1024]{1,0:T(8,128)S(1)}, u32[]{:S(2)}, u32[]{:S(2)}) %collective-permute-start.16) | collective-permute-done | bytes 262176 | tf_op jit(solution)/shard_map/ppermute | solution.py:225
  104.3 0.3 collective-permute-done.17.p4
  104.6 3.1 %shard_map.63 = f32[1024,512]{1,0:T(8,128)} custom-call(f32[256,512]{1,0:T(8,128)S(1)} %get-tuple-element.27.top, f32[256,512]{1,0:T(8,128)S(1)} %get-tuple-element.28.upper, f32[256,512]{1,0:T(8,128)S(1)} %get-tuple-element.29.lower, f32[256,512]{1,0:T(8,128)S(1)} %get-tuple-element.30.low, f32[256,512]{1,0:T(8,128)S(1)} %collective-permute-done.12.above, ...), custom_call_target="tpu_custom_call" | custom-call | flops 1610612736 | bytes 7340032 | tf_op jit(solution)/shard_map/pallas_call | solution.py:142
  (31 shorter events, 0.3 us)
Async XLA Ops:
  0.0 21.3 %copy-start.1 = (f32[2,16,512]{2,1,0:T(8,128)S(1)}, f32[2,16,512]{2,1,0:T(8,128)}, u32[]{:S(2)}) copy-start(f32[2,16,512]{2,1,0:T(8,128)} %param.8) | copy-start | bytes 196612
  2.0 19.3 %collective-permute-start = (f32[128,768]{1,0:T(8,128)S(1)}, f32[128,768]{1,0:T(8,128)S(1)}, u32[]{:S(2)}, u32[]{:S(2)}) collective-permute-start(f32[128,768]{1,0:T(8,128)S(1)} %pad_maximum_fusion.refs_0_), channel_id=1, source_target_pairs={{0,64},{32,96},{64,0},{96,32},{1,65},{33,97},{65,1},{97,33},{2,66}... | collective-permute-start | bytes 1179656 | tf_op jit(solution)/shard_map/ppermute | solution.py:26
  5.3 18.3 %all-to-all-start.1 = ((f32[8,16,1024]{2,1,0:T(8,128)}), f32[8,16,1024]{2,1,0:T(8,128)S(1)}, u32[]{:S(2)}, u32[]{:S(2)}) async-start(f32[8,16,1024]{2,1,0:T(8,128)} %broadcast_in_dim.5), calls=%async_computation.1 | async-start | bytes 1048576 | tf_op jit(solution)/shard_map/all_to_all | solution.py:219
  11.9 13.6 %collective-permute-start.3 = (f32[128,256]{1,0:T(8,128)S(1)}, f32[128,256]{1,0:T(8,128)S(1)}, u32[]{:S(2)}, u32[]{:S(2)}) collective-permute-start(f32[128,256]{1,0:T(8,128)S(1)} %get-tuple-element.31), channel_id=1, source_target_pairs={{0,31},{1,0},{2,1},{3,2},{4,3},{5,4},{6,5},{7,6},{8,7},{9,8},{10,9... | collective-permute-start | bytes 393224 | tf_op jit(solution)/shard_map/ppermute | solution.py:30
  21.0 8.2 %collective-permute-start.4 = (f32[128,256]{1,0:T(8,128)S(1)}, f32[128,256]{1,0:T(8,128)S(1)}, u32[]{:S(2)}, u32[]{:S(2)}) collective-permute-start(f32[128,256]{1,0:T(8,128)S(1)} %get-tuple-element.31), channel_id=1, source_target_pairs={{0,95},{1,64},{2,65},{3,66},{4,67},{5,68},{6,69},{7,70},{8,71},{9,... | collective-permute-start | bytes 393224 | tf_op jit(solution)/shard_map/ppermute | solution.py:212
  21.3 8.0 %collective-permute-start.2 = (f32[16,256]{1,0:T(8,128)S(1)}, f32[16,256]{1,0:T(8,128)S(1)}, u32[]{:S(2)}, u32[]{:S(2)}) collective-permute-start(f32[16,256]{1,0:T(8,128)S(1)} %get-tuple-element.35), channel_id=1, source_target_pairs={{0,96},{32,0},{64,32},{96,64},{1,97},{33,1},{65,33},{97,65},{2,98}... | collective-permute-start | bytes 49160 | tf_op jit(solution)/shard_map/ppermute | solution.py:30
  21.4 25.3 %collective-permute-start.1 = (f32[256,768]{1,0:T(8,128)S(1)}, f32[256,768]{1,0:T(8,128)S(1)}, u32[]{:S(2)}, u32[]{:S(2)}) collective-permute-start(f32[256,768]{1,0:T(8,128)S(1)} %shard_map.55.own), channel_id=1, source_target_pairs={{0,32},{32,0},{64,96},{96,64},{1,33},{33,1},{65,97},{97,65},{2,34}... | collective-permute-start | bytes 2359304 | tf_op jit(solution)/shard_map/ppermute | solution.py:26
  23.6 23.0 %copy-start = (f32[1024,512]{1,0:T(8,128)S(1)}, f32[1024,512]{1,0:T(8,128)}, u32[]{:S(2)}) copy-start(f32[1024,512]{1,0:T(8,128)} %s.1) | copy-start | bytes 6291460
  23.6 23.0 %collective-permute-start.5 = (f32[128,1024]{1,0:T(8,128)S(1)}, f32[128,1024]{1,0:T(8,128)S(1)}, u32[]{:S(2)}, u32[]{:S(2)}) collective-permute-start(f32[128,1024]{1,0:T(8,128)S(1)} %bitcast.21), channel_id=1, source_target_pairs={{0,8},{1,9},{2,10},{3,11},{4,12},{5,13},{6,14},{7,15},{8,16},{9,17... | collective-permute-start | bytes 1572872 | tf_op jit(solution)/shard_map/ppermute | solution.py:225
  25.5 21.1 %collective-permute-start.6 = (f32[128,1024]{1,0:T(8,128)S(1)}, f32[128,1024]{1,0:T(8,128)S(1)}, u32[]{:S(2)}, u32[]{:S(2)}) collective-permute-start(f32[128,1024]{1,0:T(8,128)S(1)} %bitcast.22), channel_id=1, source_target_pairs={{0,24},{1,25},{2,26},{3,27},{4,28},{5,29},{6,30},{7,31},{8,0},{9,1... | collective-permute-start | bytes 1572872 | tf_op jit(solution)/shard_map/ppermute | solution.py:225
  49.3 34.1 %collective-permute-start.7 = (f32[1024,256]{1,0:T(8,128)S(1)}, f32[1024,256]{1,0:T(8,128)S(1)}, u32[]{:S(2)}, u32[]{:S(2)}) collective-permute-start(f32[1024,256]{1,0:T(8,128)S(1)} %get-tuple-element.18.mr), channel_id=1, source_target_pairs={{0,1},{1,2},{2,3},{3,4},{4,5},{5,6},{6,7},{7,8},{8,9},{9,10},{10,1... | collective-permute-start | bytes 3145736 | tf_op jit(solution)/shard_map/ppermute | solution.py:30
  49.6 33.8 %collective-permute-start.8 = (f32[1024,256]{1,0:T(8,128)S(1)}, f32[1024,256]{1,0:T(8,128)S(1)}, u32[]{:S(2)}, u32[]{:S(2)}) collective-permute-start(f32[1024,256]{1,0:T(8,128)S(1)} %get-tuple-element.19.ml), channel_id=1, source_target_pairs={{0,31},{1,0},{2,1},{3,2},{4,3},{5,4},{6,5},{7,6},{8,7},{9,8},{10,9... | collective-permute-start | bytes 3145736 | tf_op jit(solution)/shard_map/ppermute | solution.py:30
  57.2 1.5 %collective-permute-start.9 = (f32[256,256]{1,0:T(8,128)S(1)}, f32[256,256]{1,0:T(8,128)S(1)}, u32[]{:S(2)}, u32[]{:S(2)}) collective-permute-start(f32[256,256]{1,0:T(8,128)S(1)} %shard_map.56.refs_2_.next_own), channel_id=1, source_target_pairs={{0,32},{32,0},{64,96},{96,64},{1,33},{33,1},{65,97},{97,65},{2,34}... | collective-permute-start | bytes 786440 | tf_op jit(solution)/shard_map/ppermute | solution.py:26
  60.3 23.1 %collective-permute-start.10 = (f32[64,1024]{1,0:T(8,128)S(1)}, f32[64,1024]{1,0:T(8,128)S(1)}, u32[]{:S(2)}, u32[]{:S(2)}) collective-permute-start(f32[64,1024]{1,0:T(8,128)S(1)} %get-tuple-element.25), channel_id=1, source_target_pairs={{0,8},{1,9},{2,10},{3,11},{4,12},{5,13},{6,14},{7,15},{8,16},{9,17... | collective-permute-start | bytes 786440 | tf_op jit(solution)/shard_map/ppermute | solution.py:225
  60.4 23.1 %collective-permute-start.11 = (f32[64,1024]{1,0:T(8,128)S(1)}, f32[64,1024]{1,0:T(8,128)S(1)}, u32[]{:S(2)}, u32[]{:S(2)}) collective-permute-start(f32[64,1024]{1,0:T(8,128)S(1)} %get-tuple-element.26), channel_id=1, source_target_pairs={{0,24},{1,25},{2,26},{3,27},{4,28},{5,29},{6,30},{7,31},{8,0},{9,1... | collective-permute-start | bytes 786440 | tf_op jit(solution)/shard_map/ppermute | solution.py:225
  63.6 31.0 %collective-permute-start.14 = (f32[128,1024]{1,0:T(8,128)S(1)}, f32[128,1024]{1,0:T(8,128)S(1)}, u32[]{:S(2)}, u32[]{:S(2)}) collective-permute-start(f32[128,1024]{1,0:T(8,128)S(1)} %bitcast.18), channel_id=1, source_target_pairs={{0,8},{1,9},{2,10},{3,11},{4,12},{5,13},{6,14},{7,15},{8,16},{9,17... | collective-permute-start | bytes 1572872 | tf_op jit(solution)/shard_map/ppermute | solution.py:225
  83.4 13.8 %collective-permute-start.15 = (f32[128,1024]{1,0:T(8,128)S(1)}, f32[128,1024]{1,0:T(8,128)S(1)}, u32[]{:S(2)}, u32[]{:S(2)}) collective-permute-start(f32[128,1024]{1,0:T(8,128)S(1)} %bitcast.19), channel_id=1, source_target_pairs={{0,24},{1,25},{2,26},{3,27},{4,28},{5,29},{6,30},{7,31},{8,0},{9,1... | collective-permute-start | bytes 1572872 | tf_op jit(solution)/shard_map/ppermute | solution.py:225
  84.9 19.7 %collective-permute-start.12 = (f32[256,512]{1,0:T(8,128)S(1)}, f32[256,512]{1,0:T(8,128)S(1)}, u32[]{:S(2)}, u32[]{:S(2)}) collective-permute-start(f32[256,512]{1,0:T(8,128)S(1)} %get-tuple-element.30.low), channel_id=1, source_target_pairs={{0,32},{32,64},{64,96},{96,0},{1,33},{33,65},{65,97},{97,1},{2,34}... | collective-permute-start | bytes 1572872 | tf_op jit(solution)/shard_map/ppermute | solution.py:30
  86.5 18.1 %collective-permute-start.13 = (f32[256,512]{1,0:T(8,128)S(1)}, f32[256,512]{1,0:T(8,128)S(1)}, u32[]{:S(2)}, u32[]{:S(2)}) collective-permute-start(f32[256,512]{1,0:T(8,128)S(1)} %get-tuple-element.27.top), channel_id=1, source_target_pairs={{0,96},{32,0},{64,32},{96,64},{1,97},{33,1},{65,33},{97,65},{2,98}... | collective-permute-start | bytes 1572872 | tf_op jit(solution)/shard_map/ppermute | solution.py:30
  94.6 9.7 %collective-permute-start.16 = (f32[64,1024]{1,0:T(8,128)S(1)}, f32[64,1024]{1,0:T(8,128)S(1)}, u32[]{:S(2)}, u32[]{:S(2)}) collective-permute-start(f32[64,1024]{1,0:T(8,128)S(1)} %slice.36), channel_id=1, source_target_pairs={{0,8},{1,9},{2,10},{3,11},{4,12},{5,13},{6,14},{7,15},{8,16},{9,17... | collective-permute-start | bytes 786440 | tf_op jit(solution)/shard_map/ppermute | solution.py:225
  97.2 7.4 %collective-permute-start.17 = (f32[64,1024]{1,0:T(8,128)S(1)}, f32[64,1024]{1,0:T(8,128)S(1)}, u32[]{:S(2)}, u32[]{:S(2)}) collective-permute-start(f32[64,1024]{1,0:T(8,128)S(1)} %slice.37), channel_id=1, source_target_pairs={{0,24},{1,25},{2,26},{3,27},{4,28},{5,29},{6,30},{7,31},{8,0},{9,1... | collective-permute-start | bytes 786440 | tf_op jit(solution)/shard_map/ppermute | solution.py:225
